TPU v7x, 256 devices: a whole 4x4x8 slice. The times are simulated.
256 devices in a mesh: batch: 64 (over y, x, z_hi), chan: 4 (over z_lo, core).
Axes of the slice: x: 4, y: 4, z: 8 (z_hi: 4, z_lo: 2; z = z_hi * 2 + z_lo), core: 2. Of those that a mesh axis runs over, the one named last changes fastest.
Arguments:
- fine_inputs: bfloat16 [64, 32, 32, 512], P('batch'), may hold values from -6 to 6
- fine_upstream: bfloat16 [64, 32, 32, 512], P('batch', None, None, 'chan'), may hold values from -6 to 6
- fine_bank: bfloat16 [8, 9, 512, 512], P(None, None, 'batch', 'chan'), may hold values from -0.09375 to 0.09375
- fine_coefs: float32 [64, 8], replicated, may hold values from 0 to 1, as said below
- coarse_inputs: bfloat16 [64, 16, 16, 512], P('batch'), may hold values from -6 to 6
- coarse_upstream: bfloat16 [64, 16, 16, 512], P('batch', None, None, 'chan'), may hold values from -6 to 6
- coarse_bank: bfloat16 [8, 9, 512, 512], P(None, None, 'batch', 'chan'), may hold values from -0.09375 to 0.09375
- coarse_coefs: float32 [64, 8], replicated, may hold values from 0 to 1, as said below
Outputs:
- fine_delta: bfloat16 [64, 32, 32, 512], P('batch', None, None, 'chan')
- fine_update: float32 [8, 9, 512, 512], P(None, None, 'batch', 'chan')
- fine_logit: float32 [64, 8], P('batch')
- coarse_delta: bfloat16 [64, 16, 16, 512], P('batch', None, None, 'chan')
- coarse_update: float32 [8, 9, 512, 512], P(None, None, 'batch', 'chan')
- coarse_logit: float32 [64, 8], P('batch')
Inputs may be any that keep to these rules, and one draw needn't show every extreme that they name: Each row of fine_coefs is a softmax: positive entries that sum to one. Each row of coarse_coefs is a softmax: positive entries that sum to one.
All inputs are finite; a program needn't handle non-finite values.
Results may differ from a plain program's by a relative error of at most 0.01.
Values may be sent and summed in bfloat16 or wider, within the bound.
A program may use at most 128 MiB of HBM per device.

v0:
```python
import jax
import jax.numpy as jnp
from jax import lax
from jax.sharding import PartitionSpec as P

BANKS = 8
FINE_SIDE = 32
COARSE_SIDE = 16


HIGH = lax.Precision.HIGHEST


def shifted(padded, row_shift, col_shift, side):
    window = padded[:, row_shift : row_shift + side, col_shift : col_shift + side, :]
    return window.reshape(window.shape[0], side * side, window.shape[3])


def local_grads(inputs, upstream, kernels, side):
    samples_here = inputs.shape[0]
    pad_in = jnp.pad(inputs, ((0, 0), (1, 1), (1, 1), (0, 0)))
    pad_up = jnp.pad(upstream, ((0, 0), (1, 1), (1, 1), (0, 0)))
    flat_up = upstream.reshape(samples_here, side * side, upstream.shape[3])
    delta = jnp.zeros((samples_here, side * side, inputs.shape[3]), jnp.float32)
    grad_taps = []
    for row_shift in range(3):
        for col_shift in range(3):
            tap = 3 * row_shift + col_shift
            window_in = shifted(pad_in, row_shift, col_shift, side)
            window_up = shifted(pad_up, 2 - row_shift, 2 - col_shift, side)
            grad_taps.append(
                jnp.einsum("bpc,bpo->bco", window_in, flat_up, preferred_element_type=jnp.float32)
                / side
            )
            delta = delta + jnp.einsum(
                "bpo,bco->bpc", window_up, kernels[:, tap], preferred_element_type=jnp.float32
            )
    return (delta.reshape(samples_here, side, side, inputs.shape[3]), jnp.stack(grad_taps, axis=1))


def one_layer(inputs, upstream, bank_part, coefs, side):
    samples_here = inputs.shape[0]
    first_row = lax.axis_index("batch") * samples_here
    own_coefs = lax.dynamic_slice_in_dim(coefs, first_row, samples_here, 0)
    flat_bank = bank_part.reshape(BANKS, -1).astype(jnp.float32)
    bank_rows = lax.all_gather(bank_part, "batch", axis=2, tiled=True)
    flat_rows = bank_rows.reshape(bank_rows.shape[0], -1).astype(jnp.float32)
    mixed = jnp.dot(own_coefs, flat_rows, precision=HIGH)
    kernels = mixed.reshape((samples_here,) + bank_rows.shape[1:]).astype(jnp.bfloat16)
    delta, kernel_grad = local_grads(inputs, upstream, kernels, side)
    delta_total = lax.psum(delta.astype(jnp.bfloat16), "chan").astype(jnp.float32)
    width = delta.shape[3] // lax.axis_size("chan")
    delta_part = lax.dynamic_slice_in_dim(delta_total, lax.axis_index("chan") * width, width, 3)
    moved = lax.all_to_all(
        kernel_grad.astype(jnp.bfloat16), "batch", split_axis=2, concat_axis=0, tiled=True
    ).astype(kernel_grad.dtype)
    flat_grads = moved.reshape(moved.shape[0], -1)
    update = jnp.dot(coefs.T, flat_grads, precision=HIGH).reshape(bank_part.shape)
    dcoef_part = lax.dot_general(flat_grads, flat_bank, (((1,), (1,)), ((), ())), precision=HIGH)
    return (delta_part.astype(jnp.bfloat16), update, dcoef_part)


def logit_grads(coefs, totals, samples_here):
    first_row = lax.axis_index("batch") * samples_here
    own_coefs = lax.dynamic_slice_in_dim(coefs, first_row, samples_here, 0)
    own_totals = lax.dynamic_slice_in_dim(totals, first_row, samples_here, 0)
    return own_coefs * (own_totals - jnp.sum(own_coefs * own_totals, axis=1, keepdims=True))


def per_device(
    fine_inputs,
    fine_upstream,
    fine_bank,
    fine_coefs,
    coarse_inputs,
    coarse_upstream,
    coarse_bank,
    coarse_coefs,
):
    fine_delta, fine_update, fine_partial = one_layer(
        fine_inputs, fine_upstream, fine_bank, fine_coefs, FINE_SIDE
    )
    coarse_delta, coarse_update, coarse_partial = one_layer(
        coarse_inputs, coarse_upstream, coarse_bank, coarse_coefs, COARSE_SIDE
    )
    fine_total, coarse_total = lax.psum((fine_partial, coarse_partial), ("batch", "chan"))
    samples_here = fine_inputs.shape[0]
    fine_logit = logit_grads(fine_coefs, fine_total, samples_here)
    coarse_logit = logit_grads(coarse_coefs, coarse_total, samples_here)
    return (fine_delta, fine_update, fine_logit, coarse_delta, coarse_update, coarse_logit)


def solution(mesh):
    return jax.shard_map(
        per_device,
        mesh=mesh,
        in_specs=(
            P("batch", None, None, None),
            P("batch", None, None, "chan"),
            P(None, None, "batch", "chan"),
            P(),
            P("batch", None, None, None),
            P("batch", None, None, "chan"),
            P(None, None, "batch", "chan"),
            P(),
        ),
        out_specs=(
            P("batch", None, None, "chan"),
            P(None, None, "batch", "chan"),
            P("batch", None),
            P("batch", None, None, "chan"),
            P(None, None, "batch", "chan"),
            P("batch", None),
        ),
        check_vma=False,
    )
```

profile of v0, /device:TPU:1, one launch (start us, length us, event | category | flops | bytes accessed | tf_op | source)
XLA Modules:
  0.0 524.2 jit_solution(8585332356747162847)
XLA Ops:
  7.2 0.7 all-gather.5.cloned.1.call-update
  8.0 0.7 all-gather.3.cloned.1.call-update
  8.7 1.2 fusion.60
  12.3 2.2 copy.31
  14.5 15.2 %all-to-all-start.1 = ((bf16[1,9,512,128]{3,1,0,2:T(8,128)(2,1)}), bf16[1,9,512,128]{3,1,0,2:T(8,128)(2,1)S(1)}, u32[]{:S(2)}, u32[]{:S(2)}) async-start(bf16[1,9,512,128]{3,1,0,2:T(8,128)(2,1)} %copy.31), calls=%async_computation.1 | async-start | bytes 4194304 | tf_op jit(solution)/shard_map/all_to_all | solution.py:54
  29.8 0.5 fusion.78
  30.3 0.5 fusion.76
  30.8 0.5 fusion.74
  31.4 0.5 fusion.72
  31.9 0.5 fusion.70
  32.5 0.5 fusion.68
  33.0 0.6 fusion.66
  33.6 0.5 fusion.64
  34.1 0.5 fusion.62
  34.7 2.2 copy.28
  36.9 51.0 %all-to-all-done.1 = bf16[1,9,512,128]{3,1,0,2:T(8,128)(2,1)S(1)} async-done(((bf16[1,9,512,128]{3,1,0,2:T(8,128)(2,1)}), bf16[1,9,512,128]{3,1,0,2:T(8,128)(2,1)S(1)}, u32[]{:S(2)}, u32[]{:S(2)}) %all-to-all-start.1) | async-done | bytes 1179680 | tf_op jit(solution)/shard_map/all_to_all | solution.py:54
  87.9 5.9 %all-to-all-start = ((bf16[1,9,512,128]{3,1,0,2:T(8,128)(2,1)}), bf16[1,9,512,128]{3,1,0,2:T(8,128)(2,1)}, u32[]{:S(2)}, u32[]{:S(2)}) async-start(bf16[1,9,512,128]{3,1,0,2:T(8,128)(2,1)} %copy.28), calls=%async_computation | async-start | bytes 4194304 | tf_op jit(solution)/shard_map/all_to_all | solution.py:54
  94.1 0.6 copy.41
  94.7 0.6 copy.40
  95.3 0.8 pad_slice_fusion.24
  96.1 1.3 pad_slice_fusion.16
  97.8 1.3 reshape.891
  99.1 48.8 %all-to-all-done = bf16[1,9,512,128]{3,1,0,2:T(8,128)(2,1)} async-done(((bf16[1,9,512,128]{3,1,0,2:T(8,128)(2,1)}), bf16[1,9,512,128]{3,1,0,2:T(8,128)(2,1)}, u32[]{:S(2)}, u32[]{:S(2)}) %all-to-all-start) | async-done | bytes 1179680 | tf_op jit(solution)/shard_map/all_to_all | solution.py:54
  148.0 2.0 copy.61
  150.0 0.5 reshape.858
  150.5 0.6 fusion.166
  151.1 80.3 %all-gather.5.cloned.1.call-done = bf16[8,9,512,128]{3,2,1,0:T(8,128)(2,1)} async-done(((bf16[8,9,8,128]{3,2,1,0:T(8,128)(2,1)}), bf16[8,9,512,128]{3,2,1,0:T(8,128)(2,1)}) %all-gather.5.cloned.1.call-update) | async-done | bytes 9437200 | tf_op jit(solution)/shard_map/all_gather | solution.py:46
  231.4 16.2 %copy.58 = bf16[1,8,4608,128]{3,1,2,0:T(8,128)(2,1)S(1)} copy(bf16[1,8,4608,128]{3,2,1,0:T(8,128)(2,1)} %bitcast.537) | data formatting | bytes 18874368
  247.6 8.0 %fusion.146 = f32[1,9,512,128]{3,0,2,1:T(1,128)S(1)} fusion(bf16[9,512,128,8]{2,3,1,0:T(8,128)(2,1)S(1)} %bitcast.532, f32[1,8]{0,1:T(8,128)S(1)} %get-tuple-element.44), kind=kOutput, calls=%fused_computation.215 | convolution fusion | flops 56623104 | bytes 11796512 | tf_op jit(solution)/shard_map/dot_general | solution.py:48
  255.8 136.1 %all-gather.3.cloned.1.call-done = bf16[8,9,512,128]{3,2,1,0:T(8,128)(2,1)} async-done(((bf16[8,9,8,128]{3,2,1,0:T(8,128)(2,1)}), bf16[8,9,512,128]{3,2,1,0:T(8,128)(2,1)}) %all-gather.3.cloned.1.call-update) | async-done | bytes 9437200 | tf_op jit(solution)/shard_map/all_gather | solution.py:46
  391.9 16.2 %copy.59 = bf16[1,8,4608,128]{3,1,2,0:T(8,128)(2,1)S(1)} copy(bf16[1,8,4608,128]{3,2,1,0:T(8,128)(2,1)} %bitcast.536) | data formatting | bytes 18874368
  408.1 8.3 %fusion.148 = f32[1,9,512,128]{3,0,2,1:T(1,128)S(1)} fusion(bf16[9,512,128,8]{2,3,1,0:T(8,128)(2,1)S(1)} %bitcast.533, f32[1,8]{0,1:T(8,128)S(1)} %get-tuple-element.45), kind=kOutput, calls=%fused_computation.217 | convolution fusion | flops 56623104 | bytes 11796512 | tf_op jit(solution)/shard_map/dot_general | solution.py:48
  416.6 0.8 copy-done.9
  417.3 0.4 fusion.130
  417.8 0.5 copy-done.8
  418.3 0.4 fusion.131
  418.7 0.5 copy-done.7
  419.2 0.4 fusion.133
  419.7 0.5 copy-done.6
  420.2 0.4 fusion.134
  420.6 0.5 copy-done.5
  421.1 0.4 fusion.135
  421.6 0.5 copy-done.4
  422.1 0.4 fusion.136
  422.5 0.5 copy-done.3
  423.0 0.4 fusion.129
  423.5 0.5 copy-done.2
  424.0 0.4 fusion.132
  424.4 0.4 copy-done.18
  427.9 0.9 fusion.6
  428.8 1.9 fusion.4
  430.7 1.2 copy-done
  432.0 0.6 fusion.167
  432.5 0.8 copy.33
  433.3 0.8 copy.34
  434.1 0.4 fusion.122
  434.6 0.4 fusion.125
  435.0 76.0 %all-reduce.4 = (f32[64,8]{1,0:T(8,128)S(1)}, f32[64,8]{1,0:T(8,128)S(1)}) all-reduce(f32[64,8]{1,0:T(8,128)S(1)} %fusion.125, f32[64,8]{1,0:T(8,128)S(1)} %fusion.122), channel_id=1, replica_groups=mesh['batch'=64,'chan'=4] {'batch','chan'}, use_global_device_ids=true, to_apply=%region_1.2 | all-reduce | flops 1024 | bytes 8192 | tf_op jit(solution)/shard_map/psum | solution.py:86
  511.0 0.6 multiply_reduce_fusion
  511.6 0.6 multiply_reduce_fusion.1
  512.2 1.2 subtract_multiply_fusion
  513.3 1.2 subtract_multiply_fusion.1
  514.5 1.7 convert_convert_fusion
  516.2 1.5 convert_convert_fusion.1
  (71 shorter events, 6.4 us)
Async XLA Ops:
  7.2 2.8 copy-start.10
  7.2 2.7 copy-start.27
  7.2 224.2 %all-gather.5.cloned.1.call-start = ((), (), s32[]{:S(2)}) async-start(), calls=%async_computation.3 | async-start | bytes 9584640 | tf_op jit(solution)/shard_map/all_gather | solution.py:46
  7.9 384.0 %all-gather.3.cloned.1.call-start = ((), (), s32[]{:S(2)}) async-start(), calls=%async_computation.2 | async-start | bytes 9584640 | tf_op jit(solution)/shard_map/all_gather | solution.py:46
  14.5 15.3 %copy-start.1 = (bf16[1,32,32,128]{3,2,1,0:T(8,128)(2,1)S(1)}, bf16[1,32,32,128]{3,2,1,0:T(8,128)(2,1)}, u32[]{:S(2)}) copy-start(bf16[1,32,32,128]{3,2,1,0:T(8,128)(2,1)} %param.9) | copy-start | bytes 786436
  14.5 15.3 %copy-start.26 = (bf16[1,32,32,512]{3,2,1,0:T(8,128)(2,1)S(1)}, bf16[1,32,32,512]{3,2,1,0:T(8,128)(2,1)}, u32[]{:S(2)}) copy-start(bf16[1,32,32,512]{3,2,1,0:T(8,128)(2,1)} %param.8) | copy-start | bytes 3145732
  14.5 73.4 %all-to-all-start.1 = ((bf16[1,9,512,128]{3,1,0,2:T(8,128)(2,1)}), bf16[1,9,512,128]{3,1,0,2:T(8,128)(2,1)S(1)}, u32[]{:S(2)}, u32[]{:S(2)}) async-start(bf16[1,9,512,128]{3,1,0,2:T(8,128)(2,1)} %copy.31), calls=%async_computation.1 | async-start | bytes 4194304 | tf_op jit(solution)/shard_map/all_to_all | solution.py:54
  36.9 57.2 %copy-start.22 = (f32[64,8]{0,1:T(8,128)S(1)}, f32[64,8]{0,1:T(8,128)}, u32[]{:S(2)}) copy-start(f32[64,8]{0,1:T(8,128)} %param.11) | copy-start | bytes 6148
  36.9 57.2 %copy-start.23 = (f32[64,8]{0,1:T(8,128)S(1)}, f32[64,8]{0,1:T(8,128)}, u32[]{:S(2)}) copy-start(f32[64,8]{0,1:T(8,128)} %param.15) | copy-start | bytes 6148
  87.9 60.1 %all-to-all-start = ((bf16[1,9,512,128]{3,1,0,2:T(8,128)(2,1)}), bf16[1,9,512,128]{3,1,0,2:T(8,128)(2,1)}, u32[]{:S(2)}, u32[]{:S(2)}) async-start(bf16[1,9,512,128]{3,1,0,2:T(8,128)(2,1)} %copy.28), calls=%async_computation | async-start | bytes 4194304 | tf_op jit(solution)/shard_map/all_to_all | solution.py:54
  93.8 420.7 %all-reduce.8.cloned.1.call-start = ((), (), s32[]{:S(2)}) async-start(), calls=%async_computation.4 | async-start | bytes 2621440 | tf_op jit(solution)/shard_map/psum | solution.py:51
  416.4 1.0 copy-start.9
  417.3 0.9 copy-start.8
  418.3 0.9 copy-start.7
  419.2 0.9 copy-start.6
  420.2 0.9 copy-start.5
  421.1 0.9 copy-start.4
  422.1 0.9 copy-start.3
  423.0 0.9 copy-start.2
  424.0 0.8 copy-start.18
  424.0 1.1 copy-start.17
  424.4 0.9 copy-start.16
  425.1 0.8 copy-start.15
  425.3 0.8 copy-start.11
  425.9 0.8 copy-start.14
  426.2 0.8 copy-start.13
  426.8 0.8 copy-start.12
  427.0 0.8 copy-start.19
  430.7 1.3 copy-start
  431.9 2.1 copy-start.20
  433.3 1.2 copy-start.21
  434.5 76.4 %copy-start.25 = (f32[1,8]{1,0:T(1,128)S(1)}, f32[1,8]{1,0:T(1,128)}, u32[]{:S(2)}) copy-start(f32[1,8]{1,0:T(1,128)} %copy.41) | copy-start | bytes 100
  434.5 77.0 %copy-start.24 = (f32[1,8]{1,0:T(1,128)S(1)}, f32[1,8]{1,0:T(1,128)}, u32[]{:S(2)}) copy-start(f32[1,8]{1,0:T(1,128)} %copy.40) | copy-start | bytes 100
Sparse Core Ops, SparseCore 0:
  11.1 220.1 all-gather.4
  234.5 157.3 all-gather.2
  430.8 49.6 all-reduce.7
where the time goes:
time: 525 us; the launch traced here: 524 us
  waiting for transfers between devices  318 us (61%)
  blocking collectives  76 us (14%)
  local copies, waits for them, and re-layouts  53.3 us (10%)
  matrix products  34.7 us (7%)
  starting transfers between devices  21.4 us (4%)
  between operations  14.2 us (3%)
  other arithmetic  7.02 us (1%)
    all_gather x2, waiting for transfers between devices, one_layer(): bank_rows = lax.all_gather(bank_part, 'batch', axis=2, tiled=True)  216 us
    all_to_all x2, waiting for transfers between devices, one_layer(): lax.all_to_all(kernel_grad.astype(jnp.bfloat16), 'batch', split_axis=2, c...  99.9 us
    psum x1, blocking collectives, per_device(): lax.psum((fine_partial, coarse_partial), ('batch', 'chan'))  76 us
    unnamed x62, local copies, waits for them, and re-layouts  42.3 us
    all_to_all x2, starting transfers between devices, one_layer(): lax.all_to_all(kernel_grad.astype(jnp.bfloat16), 'batch', split_axis=2, c...  21.1 us
    dot_general x2, matrix products, one_layer(): mixed = jnp.dot(own_coefs, flat_rows, precision=HIGH)  16.3 us
  transfers between devices with their start and end apart: 5, of which 4 were waited for; matrix products, arithmetic and copies ran while one was open for 10% of the time, Pallas kernels for 0%

commit v1 on v0

v1 whole, which is shorter than its diff:
```python
import functools

import jax
import jax.numpy as jnp
from jax import lax
from jax.experimental import pallas as pl
from jax.experimental.pallas import tpu as pltpu
from jax.sharding import PartitionSpec as P

BANKS = 8
TAPS = 9
CHANNELS = 512
GROUP = 128
FINE_SIDE = 32
COARSE_SIDE = 16
N_XY = 16
N_Z = 4
N_CHAN = 4
ROWS = CHANNELS // N_XY
OWN = 8
WIDE = TAPS * GROUP
ROW3 = 3 * GROUP

MESH = pl.DeviceIdType.MESH
HIGH = lax.Precision.HIGHEST
F32 = jnp.float32
BF16 = jnp.bfloat16


def iota(shape, axis):
    return lax.broadcasted_iota(jnp.int32, shape, axis)


def mm(a, b, contract, precision=None):
    dims = (((contract[0],), (contract[1],)), ((), ()))
    return lax.dot_general(a, b, dims, precision=precision, preferred_element_type=F32)


class Layer:
    def __init__(self, side, inputs, upstream, bank, coefs, delta, update, logit, scratch):
        self.side = side
        self.inputs, self.upstream, self.bank, self.coefs = inputs, upstream, bank, coefs
        self.delta, self.update, self.logit = delta, update, logit
        (
            self.shifts, self.banks, self.mix_hi, self.mix_lo, self.back_hi, self.back_lo,
            self.grad_out, self.grad_in, self.kern_out, self.kern_in,
            self.part, self.part_out, self.part_in, self.diff, self.diff_out, self.diff_in,
            self.bank_ss, self.bank_rs, self.grad_ss, self.grad_rs, self.kern_ss, self.kern_rs,
            self.part_ss, self.part_rs, self.diff_ss, self.diff_rs,
        ) = scratch


def layer_scratch(side):
    pixels = side * side
    return [
        pltpu.VMEM((pixels + 2 * side, ROW3), BF16),
        pltpu.VMEM((N_Z * BANKS * OWN, WIDE), BF16),
        pltpu.VMEM((CHANNELS, N_Z * BANKS * OWN), BF16),
        pltpu.VMEM((CHANNELS, N_Z * BANKS * OWN), BF16),
        pltpu.VMEM((N_Z * BANKS * OWN, CHANNELS), BF16),
        pltpu.VMEM((N_Z * BANKS * OWN, CHANNELS), BF16),
        pltpu.VMEM((CHANNELS, WIDE), BF16),
        pltpu.VMEM((CHANNELS, WIDE), BF16),
        pltpu.VMEM((CHANNELS, WIDE), BF16),
        pltpu.VMEM((CHANNELS, WIDE), BF16),
        pltpu.VMEM((BANKS * OWN, WIDE), F32),
        pltpu.VMEM((N_Z, BANKS * OWN, WIDE), BF16),
        pltpu.VMEM((N_Z, BANKS * OWN, WIDE), BF16),
        pltpu.VMEM((pixels, GROUP), F32),
        pltpu.VMEM((N_CHAN, pixels, GROUP), BF16),
        pltpu.VMEM((N_CHAN, pixels, GROUP), BF16),
    ] + [
        pltpu.SemaphoreType.DMA((n,))
        for n in (N_Z, N_Z, N_XY, N_XY, N_XY, N_XY, N_Z, N_Z, N_CHAN, N_CHAN)
    ]


N_LAYER_SCRATCH = 26


class Place:
    def __init__(self):
        self.batch = lax.axis_index("batch")
        self.chan = lax.axis_index("chan")
        self.xy = self.batch // N_Z
        self.z = self.batch % N_Z

    def at_xy(self, xy):
        return (xy * N_Z + self.z, self.chan)

    def at_z(self, z):
        return (self.xy * N_Z + z, self.chan)

    def at_chan(self, chan):
        return (self.batch, chan)


def rows_of(index, count):
    return pl.ds(pl.multiple_of(index * count, count), count)


def bank_copy(layer, place, z_to, z_from):
    return pltpu.make_async_remote_copy(
        src_ref=layer.banks.at[rows_of(z_from, BANKS * OWN)],
        dst_ref=layer.banks.at[rows_of(z_from, BANKS * OWN)],
        send_sem=layer.bank_ss.at[z_to],
        recv_sem=layer.bank_rs.at[z_from],
        device_id=place.at_z(z_to),
        device_id_type=MESH,
    )


def grad_copy(layer, place, xy_to, xy_from):
    return pltpu.make_async_remote_copy(
        src_ref=layer.grad_out.at[rows_of(xy_to, ROWS)],
        dst_ref=layer.grad_in.at[rows_of(xy_from, ROWS)],
        send_sem=layer.grad_ss.at[xy_to],
        recv_sem=layer.grad_rs.at[xy_from],
        device_id=place.at_xy(xy_to),
        device_id_type=MESH,
    )


def kern_copy(layer, place, xy_to, xy_from):
    return pltpu.make_async_remote_copy(
        src_ref=layer.kern_out.at[rows_of(xy_to, ROWS)],
        dst_ref=layer.kern_in.at[rows_of(xy_from, ROWS)],
        send_sem=layer.kern_ss.at[xy_to],
        recv_sem=layer.kern_rs.at[xy_from],
        device_id=place.at_xy(xy_to),
        device_id_type=MESH,
    )


def part_copy(layer, place, z_to, z_from):
    return pltpu.make_async_remote_copy(
        src_ref=layer.part_out.at[z_to],
        dst_ref=layer.part_in.at[z_from],
        send_sem=layer.part_ss.at[z_to],
        recv_sem=layer.part_rs.at[z_from],
        device_id=place.at_z(z_to),
        device_id_type=MESH,
    )


def diff_copy(layer, place, chan_to, chan_from):
    return pltpu.make_async_remote_copy(
        src_ref=layer.diff_out.at[chan_to],
        dst_ref=layer.diff_in.at[chan_from],
        send_sem=layer.diff_ss.at[chan_to],
        recv_sem=layer.diff_rs.at[chan_from],
        device_id=place.at_chan(chan_to),
        device_id_type=MESH,
    )


def coef_copy(out_ref, in_ref, send_sem, recv_sem, place, xy_to, xy_from):
    return pltpu.make_async_remote_copy(
        src_ref=out_ref.at[xy_to],
        dst_ref=in_ref.at[xy_from],
        send_sem=send_sem.at[xy_to],
        recv_sem=recv_sem.at[xy_from],
        device_id=place.at_xy(xy_to),
        device_id_type=MESH,
    )


def total_copy(ref, send_sem, recv_sem, place, chan_to, chan_from):
    return pltpu.make_async_remote_copy(
        src_ref=ref.at[chan_from],
        dst_ref=ref.at[chan_from],
        send_sem=send_sem.at[chan_to],
        recv_sem=recv_sem.at[chan_from],
        device_id=place.at_chan(chan_to),
        device_id_type=MESH,
    )


def loop(low, high, body):
    lax.fori_loop(low, high, lambda n, carry: (body(n), carry)[1], 0)


def arrange_bank(layer, place):
    for tap in range(TAPS):
        rows = layer.bank[:, tap].astype(F32).reshape(BANKS * OWN, GROUP).astype(BF16)
        layer.banks[rows_of(place.z, BANKS * OWN), tap * GROUP : (tap + 1) * GROUP] = rows


def shift_upstream(layer):
    side = layer.side
    pixels = side * side
    up = layer.upstream[...].astype(F32)
    column = iota((pixels, GROUP), 0) % side
    after = jnp.where(column < side - 1, pltpu.roll(up, pixels - 1, 0), 0.0)
    before = jnp.where(column > 0, pltpu.roll(up, 1, 0), 0.0)
    zeros = jnp.zeros((side, ROW3), BF16)
    layer.shifts[0:side] = zeros
    layer.shifts[side + pixels : 2 * side + pixels] = zeros
    for index, value in enumerate((after, up, before)):
        layer.shifts[side : side + pixels, index * GROUP : (index + 1) * GROUP] = value.astype(BF16)


def window(layer, row_shift):
    start = (2 - row_shift) * layer.side
    return layer.shifts[start : start + layer.side * layer.side]


def split(value, hi_ref, lo_ref):
    hi = value.astype(BF16)
    hi_ref[...] = hi
    lo_ref[...] = (value - hi.astype(F32)).astype(BF16)


def spread_coefs(layer, place):
    bank_rows = N_Z * BANKS * OWN
    own = layer.coefs[pl.ds(place.z, N_XY, stride=N_Z), :]
    col = iota((BANKS, bank_rows), 1)
    wide = mm(own, ((col // OWN) % BANKS == iota((BANKS, bank_rows), 0)).astype(F32), (1, 0), HIGH)
    wide = jnp.broadcast_to(wide[:, None, :], (N_XY, ROWS, bank_rows)).reshape(CHANNELS, bank_rows)
    split(jnp.where(diagonal(), wide, 0.0), layer.mix_hi, layer.mix_lo)
    col = iota((N_XY, CHANNELS), 1)
    tall = mm(own, (col // ROWS == iota((N_XY, CHANNELS), 0)).astype(F32), (0, 0), HIGH)
    tall = jnp.broadcast_to(tall[:, None, :], (BANKS, OWN, CHANNELS)).reshape(BANKS * OWN, CHANNELS)
    tall = jnp.broadcast_to(tall[None], (N_Z, BANKS * OWN, CHANNELS)).reshape(bank_rows, CHANNELS)
    row, col = iota((bank_rows, CHANNELS), 0), iota((bank_rows, CHANNELS), 1)
    same = (row // (BANKS * OWN)) * OWN + row % OWN == col % ROWS
    split(jnp.where(same, tall, 0.0), layer.back_hi, layer.back_lo)


def diagonal():
    shape = (CHANNELS, N_Z * BANKS * OWN)
    row, col = iota(shape, 0), iota(shape, 1)
    return row % ROWS == (col // (BANKS * OWN)) * OWN + col % OWN


def send_grads(layer, place):
    my_y = place.xy // 4

    def chunk(n):
        y = (my_y + 1 + n) % 4
        part = pl.ds(pl.multiple_of(y * GROUP, GROUP), GROUP)
        flipped = layer.inputs[:, part].T
        for row_shift in range(3):
            grad = mm(flipped, window(layer, row_shift), (1, 0)) * (1.0 / layer.side)
            layer.grad_out[part, row_shift * ROW3 : (row_shift + 1) * ROW3] = grad.astype(BF16)
        for x in range(4):
            to = y * 4 + (place.xy + 1 + x) % 4

            @pl.when(to != place.xy)
            def _():
                grad_copy(layer, place, to, place.xy).start()

    loop(0, 4, chunk)
    own = rows_of(place.xy, ROWS)
    layer.grad_in[own, :] = layer.grad_out[own, :]


def send_kernels(layer, place):
    my_y = place.xy // 4
    loop(1, N_Z, lambda n: bank_copy(layer, place, place.z, (place.z + n) % N_Z).wait_recv())

    def chunk(n):
        y = (my_y + 1 + n) % 4
        part = pl.ds(pl.multiple_of(y * GROUP, GROUP), GROUP)
        for row_shift in range(3):
            cols = slice(row_shift * ROW3, (row_shift + 1) * ROW3)
            banks = layer.banks[:, cols]
            mixed = mm(layer.mix_hi[part], banks, (1, 0)) + mm(layer.mix_lo[part], banks, (1, 0))
            layer.kern_out[part, cols] = mixed.astype(BF16)
        for x in range(4):
            to = y * 4 + (place.xy + 1 + x) % 4

            @pl.when(to != place.xy)
            def _():
                kern_copy(layer, place, to, place.xy).start()

    loop(0, 4, chunk)
    own = rows_of(place.xy, ROWS)
    layer.kern_in[own, :] = layer.kern_out[own, :]


def send_parts(layer, place):
    loop(1, N_XY, lambda n: grad_copy(layer, place, place.xy, (place.xy + n) % N_XY).wait_recv())

    def chunk(n):
        z = (place.z + 1 + n) % N_Z
        part = rows_of(z, BANKS * OWN)
        for row_shift in range(3):
            cols = slice(row_shift * ROW3, (row_shift + 1) * ROW3)
            grads = layer.grad_in[:, cols]
            total = mm(layer.back_hi[part], grads, (1, 0)) + mm(layer.back_lo[part], grads, (1, 0))
            layer.part[:, cols] = total
            layer.part_out[z, :, cols] = total.astype(BF16)

        @pl.when(z != place.z)
        def _():
            part_copy(layer, place, z, place.z).start()

    loop(0, N_Z, chunk)


def coef_sums(layer):
    bank_rows = N_Z * BANKS * OWN
    cross = mm(layer.grad_in[...], layer.banks[...], (1, 1))
    cross = jnp.where(diagonal(), cross, 0.0).reshape(N_XY, ROWS, bank_rows).sum(axis=1)
    row = iota((bank_rows, GROUP), 0)
    pick = ((row // OWN) % BANKS == iota((bank_rows, GROUP), 1)).astype(F32)
    return mm(cross, pick, (1, 0), HIGH)


def send_diffs(layer, place):
    def chunk(n):
        chan = (place.chan + 1 + n) % N_CHAN
        for x in range(4):
            source = chan * 4 + x

            @pl.when(source != place.xy)
            def _():
                kern_copy(layer, place, place.xy, source).wait_recv()

        part = pl.ds(pl.multiple_of(chan * GROUP, GROUP), GROUP)
        diff = mm(window(layer, 0), layer.kern_in[part, 0:ROW3], (1, 1))
        for row_shift in (1, 2):
            cols = slice(row_shift * ROW3, (row_shift + 1) * ROW3)
            diff = diff + mm(window(layer, row_shift), layer.kern_in[part, cols], (1, 1))
        layer.diff[...] = diff
        layer.diff_out[chan] = diff.astype(BF16)

        @pl.when(chan != place.chan)
        def _():
            diff_copy(layer, place, chan, place.chan).start()

    loop(0, N_CHAN, chunk)


def finish_update(layer, place):
    total = layer.part[...]
    for n in range(1, N_Z):
        source = (place.z + n) % N_Z
        part_copy(layer, place, place.z, source).wait_recv()
        total = total + layer.part_in[source].astype(F32)
    for tap in range(TAPS):
        cols = total[:, tap * GROUP : (tap + 1) * GROUP]
        layer.update[:, tap] = cols.reshape(BANKS, OWN, GROUP)


def finish_delta(layer, place):
    total = layer.diff[...]
    for n in range(1, N_CHAN):
        source = (place.chan + n) % N_CHAN
        diff_copy(layer, place, place.chan, source).wait_recv()
        total = total + layer.diff_in[source].astype(F32)
    layer.delta[...] = total.astype(BF16)


def finish_logit(layer, place, total):
    coefs = layer.coefs[pl.ds(place.batch, 1), :]
    layer.logit[...] = coefs * (total - jnp.sum(coefs * total, axis=1, keepdims=True))


def kernel(*refs):
    args, outs, scratch = refs[:8], refs[8:14], refs[14:]
    fine = Layer(FINE_SIDE, *args[:4], *outs[:3], scratch[:N_LAYER_SCRATCH])
    coarse = Layer(COARSE_SIDE, *args[4:], *outs[3:], scratch[N_LAYER_SCRATCH : 2 * N_LAYER_SCRATCH])
    coef_out, coef_in, totals, coef_ss, coef_rs, total_ss, total_rs = scratch[2 * N_LAYER_SCRATCH :]
    layers = (fine, coarse)
    place = Place()

    barrier = pltpu.get_barrier_semaphore()

    def greet(device):
        pl.semaphore_signal(barrier, inc=1, device_id=device, device_id_type=MESH)

    loop(1, N_XY, lambda n: greet(place.at_xy((place.xy + n) % N_XY)))
    loop(1, N_Z, lambda n: greet(place.at_z((place.z + n) % N_Z)))
    loop(1, N_CHAN, lambda n: greet(place.at_chan((place.chan + n) % N_CHAN)))
    for layer in layers:
        arrange_bank(layer, place)
    shift_upstream(fine)
    pl.semaphore_wait(barrier, N_XY + N_Z + N_CHAN - 3)

    for layer in layers:
        loop(1, N_Z, lambda n: bank_copy(layer, place, (place.z + n) % N_Z, place.z).start())
    send_grads(fine, place)
    shift_upstream(coarse)
    send_grads(coarse, place)
    for layer in layers:
        spread_coefs(layer, place)
    for layer in layers:
        send_kernels(layer, place)
    sums = []
    for layer in layers:
        send_parts(layer, place)
        sums.append(coef_sums(layer)[:, None, :])
    shape = (N_XY, 8, GROUP)
    level = iota(shape, 1)
    both = jnp.where(level == 0, jnp.broadcast_to(sums[0], shape), jnp.broadcast_to(sums[1], shape))
    coef_out[...] = both
    coef_sems = (coef_out, coef_in, coef_ss, coef_rs, place)
    loop(1, N_XY, lambda n: coef_copy(*coef_sems, (place.xy + n) % N_XY, place.xy).start())
    coef_in[place.xy] = coef_out[place.xy]
    for layer in layers:
        send_diffs(layer, place)
    loop(1, N_XY, lambda n: coef_copy(*coef_sems, place.xy, (place.xy + n) % N_XY).wait_recv())
    totals[place.chan] = coef_in[...].sum(axis=0)
    total_sems = (totals, total_ss, total_rs, place)
    loop(1, N_CHAN, lambda n: total_copy(*total_sems, (place.chan + n) % N_CHAN, place.chan).start())
    for layer in layers:
        finish_update(layer, place)
    for layer in layers:
        finish_delta(layer, place)
    loop(1, N_CHAN, lambda n: total_copy(*total_sems, place.chan, (place.chan + n) % N_CHAN).wait_recv())
    total = totals[...].sum(axis=0)
    for index, layer in enumerate(layers):
        finish_logit(layer, place, total[index : index + 1, 0:BANKS])

    for layer in layers:
        loop(1, N_Z, lambda n: bank_copy(layer, place, (place.z + n) % N_Z, place.z).wait_send())
        loop(1, N_XY, lambda n: grad_copy(layer, place, (place.xy + n) % N_XY, place.xy).wait_send())
        loop(1, N_XY, lambda n: kern_copy(layer, place, (place.xy + n) % N_XY, place.xy).wait_send())
        loop(1, N_Z, lambda n: part_copy(layer, place, (place.z + n) % N_Z, place.z).wait_send())
        loop(1, N_CHAN, lambda n: diff_copy(layer, place, (place.chan + n) % N_CHAN, place.chan).wait_send())
    loop(1, N_XY, lambda n: coef_copy(*coef_sems, (place.xy + n) % N_XY, place.xy).wait_send())
    loop(1, N_CHAN, lambda n: total_copy(*total_sems, (place.chan + n) % N_CHAN, place.chan).wait_send())


def per_device(
    fine_inputs,
    fine_upstream,
    fine_bank,
    fine_coefs,
    coarse_inputs,
    coarse_upstream,
    coarse_bank,
    coarse_coefs,
):
    vmem = pl.BlockSpec(memory_space=pltpu.VMEM)
    out_shape = []
    for side in (FINE_SIDE, COARSE_SIDE):
        out_shape += [
            jax.ShapeDtypeStruct((side * side, GROUP), BF16),
            jax.ShapeDtypeStruct((BANKS, TAPS, OWN, GROUP), F32),
            jax.ShapeDtypeStruct((1, BANKS), F32),
        ]
    fine_delta, fine_update, fine_logit, coarse_delta, coarse_update, coarse_logit = pl.pallas_call(
        kernel,
        out_shape=out_shape,
        in_specs=[vmem] * 8,
        out_specs=[vmem] * 6,
        scratch_shapes=layer_scratch(FINE_SIDE)
        + layer_scratch(COARSE_SIDE)
        + [
            pltpu.VMEM((N_XY, 8, GROUP), F32),
            pltpu.VMEM((N_XY, 8, GROUP), F32),
            pltpu.VMEM((N_CHAN, 8, GROUP), F32),
            pltpu.SemaphoreType.DMA((N_XY,)),
            pltpu.SemaphoreType.DMA((N_XY,)),
            pltpu.SemaphoreType.DMA((N_CHAN,)),
            pltpu.SemaphoreType.DMA((N_CHAN,)),
        ],
        compiler_params=pltpu.CompilerParams(
            collective_id=0, has_side_effects=True, vmem_limit_bytes=50 * 1024 * 1024
        ),
    )(
        fine_inputs.reshape(FINE_SIDE * FINE_SIDE, CHANNELS),
        fine_upstream.reshape(FINE_SIDE * FINE_SIDE, GROUP),
        fine_bank,
        fine_coefs,
        coarse_inputs.reshape(COARSE_SIDE * COARSE_SIDE, CHANNELS),
        coarse_upstream.reshape(COARSE_SIDE * COARSE_SIDE, GROUP),
        coarse_bank,
        coarse_coefs,
    )
    return (
        fine_delta.reshape(1, FINE_SIDE, FINE_SIDE, GROUP),
        fine_update,
        fine_logit,
        coarse_delta.reshape(1, COARSE_SIDE, COARSE_SIDE, GROUP),
        coarse_update,
        coarse_logit,
    )


def solution(mesh):
    return jax.shard_map(
        per_device,
        mesh=mesh,
        in_specs=(
            P("batch", None, None, None),
            P("batch", None, None, "chan"),
            P(None, None, "batch", "chan"),
            P(),
            P("batch", None, None, None),
            P("batch", None, None, "chan"),
            P(None, None, "batch", "chan"),
            P(),
        ),
        out_specs=(
            P("batch", None, None, "chan"),
            P(None, None, "batch", "chan"),
            P("batch", None),
            P("batch", None, None, "chan"),
            P(None, None, "batch", "chan"),
            P("batch", None),
        ),
        check_vma=False,
    )
```

time: 525 us -> 94.2 us (0.18)
  waiting for transfers between devices: 318 us -> 0 us
  Pallas kernels: 0 us -> 83 us
  blocking collectives: 76 us -> 0 us
  local copies, waits for them, and re-layouts: 53.3 us -> 10.3 us
  matrix products: 34.7 us -> 0 us
  starting transfers between devices: 21.4 us -> 0 us
  between operations: 14.2 us -> 0.66 us
  other arithmetic: 7.02 us -> 0 us
    all_gather x2 -> x0, waiting for transfers between devices: 216 us -> none  [one_layer(): bank_rows = lax.all_gather(bank_part, 'batch', axis=2, tiled=True)]
    all_to_all x2 -> x0, waiting for transfers between devices: 99.9 us -> none  [one_layer(): lax.all_to_all(kernel_grad.astype(jnp.bfloat16), 'batch', split_axis=2, c...]
    pallas_call x0 -> x1, Pallas kernels: none -> 83 us  [per_device(): pl.pallas_call(kernel, out_shape=out_shape, in_specs=[vmem] * 8, out_spec...]
    psum x1 -> x0, blocking collectives: 76 us -> none  [per_device(): lax.psum((fine_partial, coarse_partial), ('batch', 'chan'))]
    dot_general x42 -> x0, matrix products: 34.7 us -> none  [the longest x2 16.3 us: one_layer(): mixed = jnp.dot(own_coefs, flat_rows, precision=HIGH)]
    unnamed x62 -> x20, local copies, waits for them, and re-layouts: 42.3 us -> 10.3 us
    all_to_all x2 -> x0, starting transfers between devices: 21.1 us -> none  [one_layer(): lax.all_to_all(kernel_grad.astype(jnp.bfloat16), 'batch', split_axis=2, c...]
  transfers between devices with their start and end apart: 5 -> 0, of which waited for: 4 -> 0; matrix products, arithmetic and copies ran while one was open for 10% -> 0% of each run, Pallas kernels for 0% -> 0%
where the time goes in v1:
time: 94.2 us; the launch traced here: 93.9 us
  Pallas kernels  83 us (88%)
  local copies, waits for them, and re-layouts  10.3 us (11%)
    pallas_call x1, Pallas kernels, per_device(): pl.pallas_call(kernel, out_shape=out_shape, in_specs=[vmem] * 8, out_spec...  83 us
    unnamed x20, local copies, waits for them, and re-layouts  10.3 us

profile of v1, /device:TPU:1, one launch (start us, length us, event | category | flops | bytes accessed | tf_op | source)
XLA Modules:
  0.0 93.9 jit_solution(3128132354907801949)
XLA Ops:
  0.6 0.0 copy-start.5
  0.6 0.8 copy.14.refs_3_
  1.4 0.8 copy.15.refs_7_
  2.2 0.0 copy-done.5
  2.2 0.0 copy-start
  2.2 1.2 %copy-done = bf16[1,32,32,512]{3,2,1,0:T(8,128)(2,1)S(1)} copy-done((bf16[1,32,32,512]{3,2,1,0:T(8,128)(2,1)S(1)}, bf16[1,32,32,512]{3,2,1,0:T(8,128)(2,1)}, u32[]{:S(2)}) %copy-start) | copy-done | bytes 1048600
  3.4 0.0 copy-start.1
  3.4 0.9 %copy-done.1 = bf16[1,32,32,128]{3,2,1,0:T(8,128)(2,1)S(1)} copy-done((bf16[1,32,32,128]{3,2,1,0:T(8,128)(2,1)S(1)}, bf16[1,32,32,128]{3,2,1,0:T(8,128)(2,1)}, u32[]{:S(2)}) %copy-start.1) | copy-done | bytes 262168
  4.4 0.0 copy-start.2
  4.4 0.9 %copy-done.2 = bf16[1,16,16,512]{3,2,1,0:T(8,128)(2,1)S(1)} copy-done((bf16[1,16,16,512]{3,2,1,0:T(8,128)(2,1)S(1)}, bf16[1,16,16,512]{3,2,1,0:T(8,128)(2,1)}, u32[]{:S(2)}) %copy-start.2) | copy-done | bytes 262168
  5.3 0.0 copy-start.3
  5.3 0.9 copy-done.3
  6.3 0.0 copy-start.4
  6.3 0.9 copy-done.4
  7.2 83.0 %shard_map.127 = (bf16[1024,128]{1,0:T(8,128)(2,1)S(1)}, f32[8,9,8,128]{3,2,1,0:T(8,128)S(1)}, f32[1,8]{1,0:T(1,128)S(1)}, bf16[256,128]{1,0:T(8,128)(2,1)S(1)},...) custom-call(bf16[1024,512]{1,0:T(8,128)(2,1)S(1)} %bitcast.6, bf16[1024,128]{1,0:T(8,128)(2,1)S(1)} %bitcast.7, ...), custom_call_target="tpu_custom_call" | custom-call | tf_op jit(solution)/shard_map/pallas_call | solution.py:445
  90.1 0.7 copy.22
  90.8 0.7 copy.23
  91.5 0.5 copy.24
  92.1 0.6 copy.25
  92.7 0.7 copy.26
  93.4 0.5 copy.27
Async XLA Ops:
  0.6 1.6 %copy-start.5 = (bf16[1,16,16,128]{3,2,1,0:T(8,128)(2,1)S(1)}, bf16[1,16,16,128]{3,2,1,0:T(8,128)(2,1)}, u32[]{:S(2)}) copy-start(bf16[1,16,16,128]{3,2,1,0:T(8,128)(2,1)} %param.13) | copy-start | bytes 196612
  2.2 1.2 %copy-start = (bf16[1,32,32,512]{3,2,1,0:T(8,128)(2,1)S(1)}, bf16[1,32,32,512]{3,2,1,0:T(8,128)(2,1)}, u32[]{:S(2)}) copy-start(bf16[1,32,32,512]{3,2,1,0:T(8,128)(2,1)} %param.8) | copy-start | bytes 3145732
  3.4 0.9 %copy-start.1 = (bf16[1,32,32,128]{3,2,1,0:T(8,128)(2,1)S(1)}, bf16[1,32,32,128]{3,2,1,0:T(8,128)(2,1)}, u32[]{:S(2)}) copy-start(bf16[1,32,32,128]{3,2,1,0:T(8,128)(2,1)} %param.9) | copy-start | bytes 786436
  4.4 0.9 %copy-start.2 = (bf16[1,16,16,512]{3,2,1,0:T(8,128)(2,1)S(1)}, bf16[1,16,16,512]{3,2,1,0:T(8,128)(2,1)}, u32[]{:S(2)}) copy-start(bf16[1,16,16,512]{3,2,1,0:T(8,128)(2,1)} %param.12) | copy-start | bytes 786436
  5.3 0.9 copy-start.3
  6.3 0.9 copy-start.4

commit v2 on v1

v2 whole, which is shorter than its diff:
```python
import functools

import jax
import jax.numpy as jnp
from jax import lax
from jax.experimental import pallas as pl
from jax.experimental.pallas import tpu as pltpu
from jax.sharding import PartitionSpec as P

BANKS = 8
TAPS = 9
CHANNELS = 512
GROUP = 128
FINE_SIDE = 32
COARSE_SIDE = 16
SAMPLES = 64
N_XY = 16
N_Z = 4
N_CHAN = 4
ROWS = CHANNELS // N_XY
OWN = 8
WIDE = TAPS * GROUP
ROW3 = 3 * GROUP
BLOCK = BANKS * OWN
HALF = BLOCK // 2
BANK_ROWS = N_Z * BLOCK

MIB = 1024 * 1024
MESH = pl.DeviceIdType.MESH
HIGH = lax.Precision.HIGHEST
F32 = jnp.float32
BF16 = jnp.bfloat16


def iota(shape, axis):
    return lax.broadcasted_iota(jnp.int32, shape, axis)


def mm(a, b, contract, precision=None):
    dims = (((contract[0],), (contract[1],)), ((), ()))
    return lax.dot_general(a, b, dims, precision=precision, preferred_element_type=F32)


class Layer:
    def __init__(self, side, args, delta, update, logit, scratch):
        self.side, self.args = side, args
        self.delta, self.update, self.logit = delta, update, logit
        (
            self.inputs, self.upstream, self.bank, self.coefs, self.load_sem,
            self.shifts, self.banks, self.mix, self.back,
            self.grad_out, self.grad_in, self.kern_out, self.kern_in,
            self.part, self.part_out, self.part_in, self.relay, self.diff, self.diff_out, self.diff_in,
            self.bank_ss, self.bank_rs, self.grad_ss, self.grad_rs, self.kern_ss, self.kern_rs,
            self.part_ss, self.part_rs, self.diff_ss, self.diff_rs,
        ) = scratch


def layer_scratch(side):
    pixels = side * side
    return [
        pltpu.VMEM((pixels, CHANNELS), BF16),
        pltpu.VMEM((pixels, GROUP), BF16),
        pltpu.VMEM((BANKS, TAPS, OWN, GROUP), BF16),
        pltpu.VMEM((BANKS, SAMPLES), F32),
        pltpu.SemaphoreType.DMA((4,)),
        pltpu.VMEM((pixels + 2 * side, ROW3), BF16),
        pltpu.VMEM((BANK_ROWS, WIDE), BF16),
        pltpu.VMEM((2, CHANNELS, BANK_ROWS), BF16),
        pltpu.VMEM((2, BANK_ROWS, CHANNELS), BF16),
        pltpu.VMEM((CHANNELS, WIDE), BF16),
        pltpu.VMEM((CHANNELS, WIDE), BF16),
        pltpu.VMEM((CHANNELS, WIDE), BF16),
        pltpu.VMEM((CHANNELS, WIDE), BF16),
        pltpu.VMEM((N_Z, BLOCK, WIDE), F32),
        pltpu.VMEM((N_Z, BLOCK, WIDE), BF16),
        pltpu.VMEM((2, BLOCK, WIDE), BF16),
        pltpu.VMEM((2, HALF, WIDE), BF16),
        pltpu.VMEM((pixels, GROUP), F32),
        pltpu.VMEM((3, pixels, GROUP), BF16),
        pltpu.VMEM((3, pixels, GROUP), BF16),
    ] + [
        pltpu.SemaphoreType.DMA((n,))
        for n in (4, 4, 1, 1, 1, 4, 6, 6, 3, 3)
    ]


N_LAYER_SCRATCH = 30


class Place:
    def __init__(self):
        self.batch = lax.axis_index("batch")
        self.chan = lax.axis_index("chan")
        self.xy = self.batch // N_Z
        self.z = self.batch % N_Z
        self.sibling = self.chan + 1 - 2 * (self.chan % 2)
        self.across = (self.chan + 2) % N_CHAN
        self.corner = (self.sibling + 2) % N_CHAN

    def at_xy(self, xy):
        return (xy * N_Z + self.z, self.chan)

    def at_z(self, z):
        return (self.xy * N_Z + z, self.chan)

    def at_chan(self, chan):
        return (self.batch, chan)


def rows_of(index, count):
    return pl.ds(pl.multiple_of(index * count, count), count)


def bank_copy(layer, place, kind, received=False):
    step = N_Z - 1 if kind % 2 else 1
    origin = place.z if kind < 2 else (place.z + N_Z - step) % N_Z
    if received:
        origin = (origin + N_Z - step) % N_Z
    if kind < 2:
        rows = rows_of(origin, BLOCK)
    else:
        rows = rows_of(2 * origin + kind - 2, HALF)
    return pltpu.make_async_remote_copy(
        src_ref=layer.banks.at[rows],
        dst_ref=layer.banks.at[rows],
        send_sem=layer.bank_ss.at[kind],
        recv_sem=layer.bank_rs.at[kind],
        device_id=place.at_z((place.z + step) % N_Z),
        device_id_type=MESH,
    )


def grad_copy(layer, place, xy_to):
    return pltpu.make_async_remote_copy(
        src_ref=layer.grad_out.at[rows_of(xy_to, ROWS)],
        dst_ref=layer.grad_in.at[rows_of(place.xy, ROWS)],
        send_sem=layer.grad_ss.at[0],
        recv_sem=layer.grad_rs.at[0],
        device_id=place.at_xy(xy_to),
        device_id_type=MESH,
    )


def all_grads(layer, place):
    rows = pl.ds(0, (N_XY - 1) * ROWS)
    return pltpu.make_async_remote_copy(
        src_ref=layer.grad_out.at[rows],
        dst_ref=layer.grad_in.at[rows],
        send_sem=layer.grad_ss.at[0],
        recv_sem=layer.grad_rs.at[0],
        device_id=place.at_xy((place.xy + 1) % N_XY),
        device_id_type=MESH,
    )


def kern_copy(layer, place, xy_to):
    return pltpu.make_async_remote_copy(
        src_ref=layer.kern_out.at[rows_of(xy_to, ROWS)],
        dst_ref=layer.kern_in.at[rows_of(place.xy, ROWS)],
        send_sem=layer.kern_ss.at[0],
        recv_sem=layer.kern_rs.at[place.xy // 4],
        device_id=place.at_xy(xy_to),
        device_id_type=MESH,
    )


def many_kernels(layer, place, y, first, blocks):
    rows = pl.ds(pl.multiple_of(first * ROWS, ROWS), blocks * ROWS)
    return pltpu.make_async_remote_copy(
        src_ref=layer.kern_out.at[rows],
        dst_ref=layer.kern_in.at[rows],
        send_sem=layer.kern_ss.at[0],
        recv_sem=layer.kern_rs.at[y],
        device_id=place.at_xy((place.xy + 1) % N_XY),
        device_id_type=MESH,
    )


def part_copy(layer, place, kind):
    to = (place.z + (1 if kind in (0, 2, 3) else N_Z - 1)) % N_Z
    target = (place.z + 2) % N_Z if kind < 2 else to
    half = (0, 1, 1, 0, 0, 1)[kind]
    rows = pl.ds(half * HALF, HALF)
    if kind < 2:
        landing = layer.relay.at[kind]
    else:
        landing = layer.part_in.at[0 if kind < 4 else 1, rows]
    return pltpu.make_async_remote_copy(
        src_ref=layer.part_out.at[target, rows],
        dst_ref=landing,
        send_sem=layer.part_ss.at[kind],
        recv_sem=layer.part_rs.at[kind],
        device_id=place.at_z(to),
        device_id_type=MESH,
    )


def diff_copy(layer, place, kind):
    return pltpu.make_async_remote_copy(
        src_ref=layer.diff_out.at[kind],
        dst_ref=layer.diff_in.at[kind],
        send_sem=layer.diff_ss.at[kind],
        recv_sem=layer.diff_rs.at[kind],
        device_id=place.at_chan(place.across if kind == 1 else place.sibling),
        device_id_type=MESH,
    )


def coef_copy(out_ref, in_ref, send_sem, recv_sem, place, xy_to):
    return pltpu.make_async_remote_copy(
        src_ref=out_ref.at[xy_to],
        dst_ref=in_ref.at[place.xy],
        send_sem=send_sem.at[0],
        recv_sem=recv_sem.at[0],
        device_id=place.at_xy(xy_to),
        device_id_type=MESH,
    )


def all_coefs(out_ref, in_ref, send_sem, recv_sem, place):
    return pltpu.make_async_remote_copy(
        src_ref=out_ref.at[0 : N_XY - 1],
        dst_ref=in_ref.at[0 : N_XY - 1],
        send_sem=send_sem.at[0],
        recv_sem=recv_sem.at[0],
        device_id=place.at_xy((place.xy + 1) % N_XY),
        device_id_type=MESH,
    )


def total_copy(ref, send_sem, recv_sem, place, chan_to, chan_from):
    return pltpu.make_async_remote_copy(
        src_ref=ref.at[chan_from],
        dst_ref=ref.at[chan_from],
        send_sem=send_sem.at[chan_to],
        recv_sem=recv_sem.at[chan_from],
        device_id=place.at_chan(chan_to),
        device_id_type=MESH,
    )


def loop(low, high, body):
    lax.fori_loop(low, high, lambda n, carry: (body(n), carry)[1], 0)


INPUTS, UPSTREAM, BANK, COEFS = range(4)


def load(layer, which):
    held = (layer.inputs, layer.upstream, layer.bank, layer.coefs)[which]
    return pltpu.make_async_copy(layer.args[which], held, layer.load_sem.at[which])


def arrange_bank(layer, place):
    load(layer, BANK).wait()
    for tap in range(TAPS):
        rows = layer.bank[:, tap].astype(F32).reshape(BLOCK, GROUP).astype(BF16)
        layer.banks[rows_of(place.z, BLOCK), tap * GROUP : (tap + 1) * GROUP] = rows


def shift_upstream(layer):
    load(layer, UPSTREAM).wait()
    side = layer.side
    pixels = side * side
    up = layer.upstream[...].astype(F32)
    column = iota((pixels, GROUP), 0) & (side - 1)
    after = jnp.where(column < side - 1, pltpu.roll(up, pixels - 1, 0), 0.0)
    before = jnp.where(column > 0, pltpu.roll(up, 1, 0), 0.0)
    zeros = jnp.zeros((side, ROW3), BF16)
    layer.shifts[0:side] = zeros
    layer.shifts[side + pixels : 2 * side + pixels] = zeros
    for index, value in enumerate((after, up, before)):
        layer.shifts[side : side + pixels, index * GROUP : (index + 1) * GROUP] = value.astype(BF16)


def window(layer, row_shift):
    start = (2 - row_shift) * layer.side
    return layer.shifts[start : start + layer.side * layer.side]


def split(value, ref):
    hi = value.astype(BF16)
    ref[0] = hi
    ref[1] = (value - hi.astype(F32)).astype(BF16)


def spread_coefs(layer, place):
    load(layer, COEFS).wait()
    bank_rows = BANK_ROWS
    chosen = iota((SAMPLES, N_XY), 0) == iota((SAMPLES, N_XY), 1) * N_Z + place.z
    own = mm(layer.coefs[...], chosen.astype(F32), (1, 0), HIGH)
    col = iota((BANKS, bank_rows), 1)
    wide = mm(own, ((col // OWN) % BANKS == iota((BANKS, bank_rows), 0)).astype(F32), (0, 0), HIGH)
    wide = jnp.broadcast_to(wide[:, None, :], (N_XY, ROWS, bank_rows)).reshape(CHANNELS, bank_rows)
    split(jnp.where(diagonal(), wide, 0.0), layer.mix)
    col = iota((N_XY, CHANNELS), 1)
    tall = mm(own, (col // ROWS == iota((N_XY, CHANNELS), 0)).astype(F32), (1, 0), HIGH)
    tall = jnp.broadcast_to(tall[:, None, :], (BANKS, OWN, CHANNELS)).reshape(BLOCK, CHANNELS)
    tall = jnp.broadcast_to(tall[None], (N_Z, BLOCK, CHANNELS)).reshape(bank_rows, CHANNELS)
    row, col = iota((bank_rows, CHANNELS), 0), iota((bank_rows, CHANNELS), 1)
    same = (row // (BLOCK)) * OWN + row % OWN == col % ROWS
    split(jnp.where(same, tall, 0.0), layer.back)


def diagonal():
    shape = (CHANNELS, BANK_ROWS)
    row, col = iota(shape, 0), iota(shape, 1)
    return row % ROWS == (col // (BLOCK)) * OWN + col % OWN


def send_rows(place, copy):
    my_y = place.xy // 4

    def some(n):
        y = (my_y + n // 4) % 4
        copy(y * 4 + (place.xy + n) % 4).start()

    loop(1, N_XY, some)


def send_grads(layer, place):
    load(layer, INPUTS).wait()

    def chunk(n):
        part = pl.ds(pl.multiple_of(n * 2 * GROUP, 2 * GROUP), 2 * GROUP)
        flipped = layer.inputs[:, part].T
        for row_shift in range(3):
            grad = mm(flipped, window(layer, row_shift), (1, 0)) * (1.0 / layer.side)
            layer.grad_out[part, row_shift * ROW3 : (row_shift + 1) * ROW3] = grad.astype(BF16)

    loop(0, 2, chunk)
    send_rows(place, functools.partial(grad_copy, layer, place))
    own = rows_of(place.xy, ROWS)
    layer.grad_in[own, :] = layer.grad_out[own, :]


def forward_bank(layer, place):
    for kind in (0, 1):
        bank_copy(layer, place, kind, received=True).wait_recv()
        bank_copy(layer, place, kind + 2).start()


def send_kernels(layer, place):
    for kind in (2, 3):
        bank_copy(layer, place, kind, received=True).wait_recv()
    for row_shift in range(3):
        cols = slice(row_shift * ROW3, (row_shift + 1) * ROW3)
        banks = layer.banks[:, cols]

        def chunk(n):
            part = pl.ds(pl.multiple_of(n * 2 * GROUP, 2 * GROUP), 2 * GROUP)
            mixed = mm(layer.mix[0, part], banks, (1, 0)) + mm(layer.mix[1, part], banks, (1, 0))
            layer.kern_out[part, cols] = mixed.astype(BF16)

        loop(0, 2, chunk)
    send_rows(place, functools.partial(kern_copy, layer, place))
    own = rows_of(place.xy, ROWS)
    layer.kern_in[own, :] = layer.kern_out[own, :]


def send_parts(layer, place):
    all_grads(layer, place).wait_recv()
    for row_shift in range(3):
        cols = slice(row_shift * ROW3, (row_shift + 1) * ROW3)
        grads = layer.grad_in[:, cols]
        total = mm(layer.back[0], grads, (1, 0)) + mm(layer.back[1], grads, (1, 0))
        total = total.reshape(N_Z, BLOCK, ROW3)
        layer.part[:, :, cols] = total
        layer.part_out[:, :, cols] = total.astype(BF16)
    for kind in (0, 1, 2, 4):
        part_copy(layer, place, kind).start()


def relay_parts(layer, place):
    for kind, half in ((0, 0), (1, 1)):
        part_copy(layer, place, kind).wait_recv()
        target = (place.z + (1 if kind == 0 else N_Z - 1)) % N_Z
        rows = slice(half * HALF, (half + 1) * HALF)
        total = layer.part[target, rows] + layer.relay[kind].astype(F32)
        layer.part_out[target, rows] = total.astype(BF16)
        part_copy(layer, place, 3 if kind == 0 else 5).start()


def coef_sums(layer):
    bank_rows = BANK_ROWS
    cross = mm(layer.grad_in[...], layer.banks[...], (1, 1))
    cross = jnp.where(diagonal(), cross, 0.0).reshape(N_XY, ROWS, bank_rows).sum(axis=1)
    row = iota((bank_rows, GROUP), 0)
    pick = ((row // OWN) % BANKS == iota((bank_rows, GROUP), 1)).astype(F32)
    return mm(cross, pick, (1, 0), HIGH)


def diff_of(layer, place, chan):
    y, my_y = chan, place.xy // 4

    @pl.when(y != my_y)
    def _():
        many_kernels(layer, place, y, y * 4, 4).wait_recv()

    @pl.when(y == my_y)
    def _():
        many_kernels(layer, place, y, y * 4, 3).wait_recv()

    part = pl.ds(pl.multiple_of(chan * GROUP, GROUP), GROUP)
    diff = mm(window(layer, 0), layer.kern_in[part, 0:ROW3], (1, 1))
    for row_shift in (1, 2):
        cols = slice(row_shift * ROW3, (row_shift + 1) * ROW3)
        diff = diff + mm(window(layer, row_shift), layer.kern_in[part, cols], (1, 1))
    layer.diff[...] = diff


def send_diffs(layer, place):
    diff_of(layer, place, place.corner)
    layer.diff_out[0] = layer.diff[...].astype(BF16)
    diff_copy(layer, place, 0).start()
    diff_of(layer, place, place.across)
    diff_copy(layer, place, 0).wait_recv()
    layer.diff_out[1] = (layer.diff[...] + layer.diff_in[0].astype(F32)).astype(BF16)
    diff_copy(layer, place, 1).start()
    diff_of(layer, place, place.sibling)
    layer.diff_out[2] = layer.diff[...].astype(BF16)
    diff_copy(layer, place, 2).start()
    diff_of(layer, place, place.chan)


def finish_update(layer, place):
    for kind in (2, 3, 4, 5):
        part_copy(layer, place, kind).wait_recv()
    total = layer.part[place.z] + layer.part_in[0].astype(F32) + layer.part_in[1].astype(F32)
    for tap in range(TAPS):
        cols = total[:, tap * GROUP : (tap + 1) * GROUP]
        layer.update[:, tap] = cols.reshape(BANKS, OWN, GROUP)


def finish_delta(layer, place):
    total = layer.diff[...]
    for kind in (2, 1):
        diff_copy(layer, place, kind).wait_recv()
        total = total + layer.diff_in[kind].astype(F32)
    layer.delta[...] = total.astype(BF16)


def finish_logit(layer, place, total):
    chosen = (iota((1, SAMPLES), 1) == place.batch).astype(F32)
    coefs = mm(chosen, layer.coefs[...], (1, 1), HIGH)
    layer.logit[...] = coefs * (total - jnp.sum(coefs * total, axis=1, keepdims=True))


def kernel(*refs):
    args, outs, scratch = refs[:8], refs[8:14], refs[14:]
    fine = Layer(FINE_SIDE, args[:4], *outs[:3], scratch[:N_LAYER_SCRATCH])
    coarse = Layer(COARSE_SIDE, args[4:], *outs[3:], scratch[N_LAYER_SCRATCH : 2 * N_LAYER_SCRATCH])
    coef_out, coef_in, totals, coef_ss, coef_rs, total_ss, total_rs = scratch[2 * N_LAYER_SCRATCH :]
    layers = (fine, coarse)
    place = Place()

    for which in (BANK, UPSTREAM, INPUTS, COEFS):
        for layer in layers:
            load(layer, which).start()
    barrier = pltpu.get_barrier_semaphore()

    def greet(device):
        pl.semaphore_signal(barrier, inc=1, device_id=device, device_id_type=MESH)

    loop(1, N_XY, lambda n: greet(place.at_xy((place.xy + n) % N_XY)))
    for step in (1, N_Z - 1):
        greet(place.at_z((place.z + step) % N_Z))
    loop(1, N_CHAN, lambda n: greet(place.at_chan((place.chan + n) % N_CHAN)))
    for layer in layers:
        arrange_bank(layer, place)
    shift_upstream(fine)
    pl.semaphore_wait(barrier, N_XY + N_CHAN)

    for layer in layers:
        for kind in (0, 1):
            bank_copy(layer, place, kind).start()
    send_grads(fine, place)
    forward_bank(fine, place)
    shift_upstream(coarse)
    send_grads(coarse, place)
    forward_bank(coarse, place)
    for layer in layers:
        spread_coefs(layer, place)
    for layer in layers:
        send_kernels(layer, place)
    send_parts(fine, place)
    fine_sums = coef_sums(fine)
    send_parts(coarse, place)
    relay_parts(fine, place)
    coarse_sums = coef_sums(coarse)
    shape = (N_XY, 8, GROUP)
    wide_sums = [jnp.broadcast_to(sums[:, None, :], shape) for sums in (fine_sums, coarse_sums)]
    coef_out[...] = jnp.where(iota(shape, 1) == 0, *wide_sums)
    coef_refs = (coef_out, coef_in, coef_ss, coef_rs, place)
    loop(1, N_XY, lambda n: coef_copy(*coef_refs, (place.xy + n) % N_XY).start())
    coef_in[place.xy] = coef_out[place.xy]
    relay_parts(coarse, place)
    all_coefs(*coef_refs).wait_recv()
    totals[place.chan] = coef_in[...].sum(axis=0)
    total_refs = (totals, total_ss, total_rs, place)
    loop(1, N_CHAN, lambda n: total_copy(*total_refs, (place.chan + n) % N_CHAN, place.chan).start())
    send_diffs(fine, place)
    for layer in layers:
        finish_update(layer, place)
    loop(1, N_CHAN, lambda n: total_copy(*total_refs, place.chan, (place.chan + n) % N_CHAN).wait_recv())
    total = totals[...].sum(axis=0)
    for index, layer in enumerate(layers):
        finish_logit(layer, place, total[index : index + 1, 0:BANKS])
    send_diffs(coarse, place)
    for layer in layers:
        finish_delta(layer, place)

    for layer in layers:
        for kind in range(4):
            bank_copy(layer, place, kind).wait_send()
        for kind in range(6):
            part_copy(layer, place, kind).wait_send()
        for kind in range(3):
            diff_copy(layer, place, kind).wait_send()
        all_grads(layer, place).wait_send()
        many_kernels(layer, place, 0, 0, N_XY - 1).wait_send()
    all_coefs(*coef_refs).wait_send()
    loop(1, N_CHAN, lambda n: total_copy(*total_refs, (place.chan + n) % N_CHAN, place.chan).wait_send())


def store(*refs):
    given, out, held, (in_sem, out_sem) = refs[:6], refs[6:12], refs[12:18], refs[18:]
    loads = [pltpu.make_async_copy(given[n], held[n], in_sem.at[n]) for n in range(6)]
    stores = [pltpu.make_async_copy(held[n], out[n], out_sem.at[n]) for n in range(6)]
    for copy in loads:
        copy.start()
    for first, second in zip(loads, stores):
        first.wait()
        second.start()
    for copy in stores:
        copy.wait()


def per_device(
    fine_inputs,
    fine_upstream,
    fine_bank,
    fine_coefs,
    coarse_inputs,
    coarse_upstream,
    coarse_bank,
    coarse_coefs,
):
    vmem = pl.BlockSpec(memory_space=pltpu.VMEM)
    hbm = pl.BlockSpec(memory_space=pltpu.HBM)
    out_shape = []
    for side in (FINE_SIDE, COARSE_SIDE):
        out_shape += [
            jax.ShapeDtypeStruct((side * side, GROUP), BF16),
            jax.ShapeDtypeStruct((BANKS, TAPS, OWN, GROUP), F32),
            jax.ShapeDtypeStruct((1, BANKS), F32),
        ]
    results = pl.pallas_call(
        kernel,
        out_shape=out_shape,
        in_specs=[hbm] * 8,
        out_specs=[vmem] * 6,
        scratch_shapes=layer_scratch(FINE_SIDE)
        + layer_scratch(COARSE_SIDE)
        + [
            pltpu.VMEM((N_XY, 8, GROUP), F32),
            pltpu.VMEM((N_XY, 8, GROUP), F32),
            pltpu.VMEM((N_CHAN, 8, GROUP), F32),
            pltpu.SemaphoreType.DMA((1,)),
            pltpu.SemaphoreType.DMA((1,)),
            pltpu.SemaphoreType.DMA((N_CHAN,)),
            pltpu.SemaphoreType.DMA((N_CHAN,)),
        ],
        compiler_params=pltpu.CompilerParams(
            collective_id=0, has_side_effects=True, vmem_limit_bytes=62 * MIB
        ),
    )(
        fine_inputs.reshape(FINE_SIDE * FINE_SIDE, CHANNELS),
        fine_upstream.reshape(FINE_SIDE * FINE_SIDE, GROUP),
        fine_bank,
        fine_coefs.T,
        coarse_inputs.reshape(COARSE_SIDE * COARSE_SIDE, CHANNELS),
        coarse_upstream.reshape(COARSE_SIDE * COARSE_SIDE, GROUP),
        coarse_bank,
        coarse_coefs.T,
    )
    fine_delta, fine_update, fine_logit, coarse_delta, coarse_update, coarse_logit = pl.pallas_call(
        store,
        out_shape=out_shape,
        in_specs=[hbm] * 6,
        out_specs=[hbm] * 6,
        scratch_shapes=[pltpu.VMEM(out.shape, out.dtype) for out in out_shape]
        + [pltpu.SemaphoreType.DMA((6,)), pltpu.SemaphoreType.DMA((6,))],
        compiler_params=pltpu.CompilerParams(vmem_limit_bytes=62 * MIB),
    )(*results)
    return (
        fine_delta.reshape(1, FINE_SIDE, FINE_SIDE, GROUP),
        fine_update,
        fine_logit,
        coarse_delta.reshape(1, COARSE_SIDE, COARSE_SIDE, GROUP),
        coarse_update,
        coarse_logit,
    )


def solution(mesh):
    return jax.shard_map(
        per_device,
        mesh=mesh,
        in_specs=(
            P("batch", None, None, None),
            P("batch", None, None, "chan"),
            P(None, None, "batch", "chan"),
            P(),
            P("batch", None, None, None),
            P("batch", None, None, "chan"),
            P(None, None, "batch", "chan"),
            P(),
        ),
        out_specs=(
            P("batch", None, None, "chan"),
            P(None, None, "batch", "chan"),
            P("batch", None),
            P("batch", None, None, "chan"),
            P(None, None, "batch", "chan"),
            P("batch", None),
        ),
        check_vma=False,
    )
```

time: 94.2 us -> 86 us (0.913)
  local copies, waits for them, and re-layouts: 10.3 us -> 0 us
  Pallas kernels: 83 us -> 85.2 us
    unnamed x20 -> x0, local copies, waits for them, and re-layouts: 10.3 us -> none
    pallas_call x1 -> x2, Pallas kernels: 83 us -> 85.2 us  [the longest x1 83.2 us: per_device(): pl.pallas_call(kernel, out_shape=out_shape, in_specs=[hbm] * 8, out_specs...]
where the time goes in v2:
time: 86 us; the launch traced here: 85.8 us
  Pallas kernels  85.2 us (99%)
    pallas_call x1, Pallas kernels, per_device(): pl.pallas_call(kernel, out_shape=out_shape, in_specs=[hbm] * 8, out_specs...  83.2 us
    pallas_call x1, Pallas kernels, per_device(): pl.pallas_call(store, out_shape=out_shape, in_specs=[hbm] * 6, out_specs=...  1.99 us

profile of v2, /device:TPU:1, one launch (start us, length us, event | category | flops | bytes accessed | tf_op | source)
XLA Modules:
  0.0 85.8 jit_solution(16747817282487002777)
XLA Ops:
  0.6 83.2 %shard_map.127 = (bf16[1024,128]{1,0:T(8,128)(2,1)}, f32[8,9,8,128]{3,2,1,0:T(8,128)}, f32[1,8]{1,0:T(1,128)}, bf16[256,128]{1,0:T(8,128)(2,1)}, f32[8,9,8,128]{3,2,1,0:T(8,128)}, /*index=5*/f32[1,8]{1,0:T(1,128)}) custom-call(bf16[1024,512]{1,0:T(8,128)(2,1)} %bitcast.8, bf16[1024,128]{1,0:T(8,128)(2,1)} %bitcast.9, bf16[8,9,8,128]{3,2,1,0:T(8,128)(2,1)} %refs_2_.1, ...), custom_call_target="tpu_custom_call" | custom-call | tf_op jit(solution)/shard_map/pallas_call | solution.py:558
  83.9 2.0 %shard_map.128 = (bf16[1024,128]{1,0:T(8,128)(2,1)}, f32[8,9,8,128]{3,2,1,0:T(8,128)}, f32[1,8]{1,0:T(1,128)}, bf16[256,128]{1,0:T(8,128)(2,1)}, f32[8,9,8,128]{3,2,1,0:T(8,128)}, /*index=5*/f32[1,8]{1,0:T(1,128)}) custom-call(bf16[1024,128]{1,0:T(8,128)(2,1)} %get-tuple-element.18.refs_0_, f32[8,9,8,128]{3,2,1,0:T(8,128)} %get-tuple-element.19.refs_1_, ...), custom_call_target="tpu_custom_call" | custom-call | tf_op jit(solution)/shard_map/pallas_call | solution.py:587

commit v3 on v2

--- a/solution.py
+++ b/solution.py
@@ -13,6 +13,8 @@
 GROUP = 128
 FINE_SIDE = 32
 COARSE_SIDE = 16
+STEP = 128
+AT_ONCE = 4
 SAMPLES = 64
 N_XY = 16
 N_Z = 4
@@ -47,7 +49,7 @@
         self.delta, self.update, self.logit = delta, update, logit
         (
             self.inputs, self.upstream, self.bank, self.coefs, self.load_sem,
-            self.shifts, self.banks, self.mix, self.back,
+            self.shifts, self.flipped, self.spread, self.cross, self.banks, self.mix, self.back,
             self.grad_out, self.grad_in, self.kern_out, self.kern_in,
             self.part, self.part_out, self.part_in, self.relay, self.diff, self.diff_out, self.diff_in,
             self.bank_ss, self.bank_rs, self.grad_ss, self.grad_rs, self.kern_ss, self.kern_rs,
@@ -57,6 +59,7 @@
 
 def layer_scratch(side):
     pixels = side * side
+    diff = (pixels, GROUP) if side == FINE_SIDE else (GROUP, pixels)
     return [
         pltpu.VMEM((pixels, CHANNELS), BF16),
         pltpu.VMEM((pixels, GROUP), BF16),
@@ -64,6 +67,9 @@
         pltpu.VMEM((BANKS, SAMPLES), F32),
         pltpu.SemaphoreType.DMA((4,)),
         pltpu.VMEM((pixels + 2 * side, ROW3), BF16),
+        pltpu.VMEM((CHANNELS, pixels), BF16),
+        pltpu.VMEM((N_XY, BANK_ROWS), F32),
+        pltpu.VMEM((N_XY, BANK_ROWS), F32),
         pltpu.VMEM((BANK_ROWS, WIDE), BF16),
         pltpu.VMEM((2, CHANNELS, BANK_ROWS), BF16),
         pltpu.VMEM((2, BANK_ROWS, CHANNELS), BF16),
@@ -75,16 +81,16 @@
         pltpu.VMEM((N_Z, BLOCK, WIDE), BF16),
         pltpu.VMEM((2, BLOCK, WIDE), BF16),
         pltpu.VMEM((2, HALF, WIDE), BF16),
-        pltpu.VMEM((pixels, GROUP), F32),
-        pltpu.VMEM((3, pixels, GROUP), BF16),
-        pltpu.VMEM((3, pixels, GROUP), BF16),
+        pltpu.VMEM(diff, F32),
+        pltpu.VMEM((3, *diff), BF16),
+        pltpu.VMEM((3, *diff), BF16),
     ] + [
         pltpu.SemaphoreType.DMA((n,))
         for n in (4, 4, 1, 1, 1, 4, 6, 6, 3, 3)
     ]
 
 
-N_LAYER_SCRATCH = 30
+N_LAYER_SCRATCH = 33
 
 
 class Place:
@@ -95,7 +101,6 @@
         self.z = self.batch % N_Z
         self.sibling = self.chan + 1 - 2 * (self.chan % 2)
         self.across = (self.chan + 2) % N_CHAN
-        self.corner = (self.sibling + 2) % N_CHAN
 
     def at_xy(self, xy):
         return (xy * N_Z + self.z, self.chan)
@@ -253,82 +258,110 @@
 
 def arrange_bank(layer, place):
     load(layer, BANK).wait()
-    for tap in range(TAPS):
+
+    def move(tap):
         rows = layer.bank[:, tap].astype(F32).reshape(BLOCK, GROUP).astype(BF16)
-        layer.banks[rows_of(place.z, BLOCK), tap * GROUP : (tap + 1) * GROUP] = rows
+        layer.banks[rows_of(place.z, BLOCK), rows_of(tap, GROUP)] = rows
+
+    loop(0, TAPS, move)
+
+
+def clear_edges(shifts, side):
+    zeros = jnp.zeros((side, ROW3), BF16)
+    shifts[0:side] = zeros
+    shifts[shifts.shape[0] - side : shifts.shape[0]] = zeros
+
+
+def shift_rows(upstream, shifts, side, n):
+    column = iota((STEP, GROUP), 0) & (side - 1)
+    up = upstream[rows_of(n, STEP)].astype(F32)
+    after = jnp.where(column < side - 1, pltpu.roll(up, STEP - 1, 0), 0.0)
+    before = jnp.where(column > 0, pltpu.roll(up, 1, 0), 0.0)
+    rows = pl.ds(pl.multiple_of(n * STEP + side, side), STEP)
+    for index, value in enumerate((after, up, before)):
+        shifts[rows, index * GROUP : (index + 1) * GROUP] = value.astype(BF16)
 
 
 def shift_upstream(layer):
     load(layer, UPSTREAM).wait()
-    side = layer.side
-    pixels = side * side
-    up = layer.upstream[...].astype(F32)
-    column = iota((pixels, GROUP), 0) & (side - 1)
-    after = jnp.where(column < side - 1, pltpu.roll(up, pixels - 1, 0), 0.0)
-    before = jnp.where(column > 0, pltpu.roll(up, 1, 0), 0.0)
-    zeros = jnp.zeros((side, ROW3), BF16)
-    layer.shifts[0:side] = zeros
-    layer.shifts[side + pixels : 2 * side + pixels] = zeros
-    for index, value in enumerate((after, up, before)):
-        layer.shifts[side : side + pixels, index * GROUP : (index + 1) * GROUP] = value.astype(BF16)
-
-
-def window(layer, row_shift):
-    start = (2 - row_shift) * layer.side
-    return layer.shifts[start : start + layer.side * layer.side]
-
-
-def split(value, ref):
+    clear_edges(layer.shifts, layer.side)
+    loop(0, layer.side * layer.side // STEP, lambda n: shift_rows(layer.upstream, layer.shifts, layer.side, n))
+
+
+def window(layer, row_shift, first, count):
+    start = pl.multiple_of((2 - row_shift) * layer.side + first, layer.side)
+    return layer.shifts[pl.ds(start, count)]
+
+
+def split(value, ref, rows):
     hi = value.astype(BF16)
-    ref[0] = hi
-    ref[1] = (value - hi.astype(F32)).astype(BF16)
+    ref[0, rows] = hi
+    ref[1, rows] = (value - hi.astype(F32)).astype(BF16)
 
 
 def spread_coefs(layer, place):
     load(layer, COEFS).wait()
-    bank_rows = BANK_ROWS
     chosen = iota((SAMPLES, N_XY), 0) == iota((SAMPLES, N_XY), 1) * N_Z + place.z
     own = mm(layer.coefs[...], chosen.astype(F32), (1, 0), HIGH)
-    col = iota((BANKS, bank_rows), 1)
-    wide = mm(own, ((col // OWN) % BANKS == iota((BANKS, bank_rows), 0)).astype(F32), (0, 0), HIGH)
-    wide = jnp.broadcast_to(wide[:, None, :], (N_XY, ROWS, bank_rows)).reshape(CHANNELS, bank_rows)
-    split(jnp.where(diagonal(), wide, 0.0), layer.mix)
+    col = iota((BANKS, BANK_ROWS), 1)
+    wide = ((col // OWN) % BANKS == iota((BANKS, BANK_ROWS), 0)).astype(F32)
+    layer.spread[...] = mm(own, wide, (0, 0), HIGH)
+    same = diagonal(ROWS)
+
+    def sample(n):
+        row = jnp.broadcast_to(layer.spread[pl.ds(n, 1), :], (ROWS, BANK_ROWS))
+        split(jnp.where(same, row, 0.0), layer.mix, rows_of(n, ROWS))
+
+    loop(0, N_XY, sample)
     col = iota((N_XY, CHANNELS), 1)
     tall = mm(own, (col // ROWS == iota((N_XY, CHANNELS), 0)).astype(F32), (1, 0), HIGH)
     tall = jnp.broadcast_to(tall[:, None, :], (BANKS, OWN, CHANNELS)).reshape(BLOCK, CHANNELS)
-    tall = jnp.broadcast_to(tall[None], (N_Z, BLOCK, CHANNELS)).reshape(bank_rows, CHANNELS)
-    row, col = iota((bank_rows, CHANNELS), 0), iota((bank_rows, CHANNELS), 1)
-    same = (row // (BLOCK)) * OWN + row % OWN == col % ROWS
-    split(jnp.where(same, tall, 0.0), layer.back)
-
-
-def diagonal():
-    shape = (CHANNELS, BANK_ROWS)
+    row, col = iota((BLOCK, CHANNELS), 0), iota((BLOCK, CHANNELS), 1)
+
+    def block(n):
+        same = n * OWN + row % OWN == col % ROWS
+        split(jnp.where(same, tall, 0.0), layer.back, rows_of(n, BLOCK))
+
+    loop(0, N_Z, block)
+
+
+def diagonal(rows):
+    shape = (rows, BANK_ROWS)
     row, col = iota(shape, 0), iota(shape, 1)
-    return row % ROWS == (col // (BLOCK)) * OWN + col % OWN
+    return row % ROWS == (col // BLOCK) * OWN + col % OWN
+
+
+AROUND = (
+    (1, 0), (0, 1), (3, 0), (0, 3), (1, 1), (3, 3), (2, 0), (0, 2),
+    (1, 3), (3, 1), (2, 1), (2, 3), (1, 2), (3, 2), (2, 2),
+)
 
 
 def send_rows(place, copy):
-    my_y = place.xy // 4
-
-    def some(n):
-        y = (my_y + n // 4) % 4
-        copy(y * 4 + (place.xy + n) % 4).start()
-
-    loop(1, N_XY, some)
+    y, x = place.xy // 4, place.xy % 4
+    for step_x, step_y in AROUND:
+        copy((y + step_y) % 4 * 4 + (x + step_x) % 4).start()
+
+
+def flip_inputs(layer):
+    load(layer, INPUTS).wait()
+
+    def flip(n):
+        layer.flipped[rows_of(n, GROUP)] = layer.inputs[:, rows_of(n, GROUP)].T
+
+    loop(0, CHANNELS // GROUP, flip)
 
 
 def send_grads(layer, place):
-    load(layer, INPUTS).wait()
+    flip_inputs(layer)
+    pixels = layer.side * layer.side
 
     def chunk(n):
-        part = pl.ds(pl.multiple_of(n * 2 * GROUP, 2 * GROUP), 2 * GROUP)
-        flipped = layer.inputs[:, part].T
-        for row_shift in range(3):
-            grad = mm(flipped, window(layer, row_shift), (1, 0)) * (1.0 / layer.side)
-            layer.grad_out[part, row_shift * ROW3 : (row_shift + 1) * ROW3] = grad.astype(BF16)
-
-    loop(0, 2, chunk)
+        row_shift, part = n // 2, rows_of(n % 2, 2 * GROUP)
+        grad = mm(layer.flipped[part], window(layer, row_shift, 0, pixels), (1, 0)) * (1.0 / layer.side)
+        layer.grad_out[part, rows_of(row_shift, ROW3)] = grad.astype(BF16)
+
+    loop(0, 6, chunk)
     send_rows(place, functools.partial(grad_copy, layer, place))
     own = rows_of(place.xy, ROWS)
     layer.grad_in[own, :] = layer.grad_out[own, :]
@@ -340,33 +373,114 @@
         bank_copy(layer, place, kind + 2).start()
 
 
-def send_kernels(layer, place):
+def mix_kernels(layer, place):
     for kind in (2, 3):
         bank_copy(layer, place, kind, received=True).wait_recv()
-    for row_shift in range(3):
-        cols = slice(row_shift * ROW3, (row_shift + 1) * ROW3)
+
+    def chunk(n):
+        cols, part = rows_of(n // 2, ROW3), rows_of(n % 2, 2 * GROUP)
         banks = layer.banks[:, cols]
-
-        def chunk(n):
-            part = pl.ds(pl.multiple_of(n * 2 * GROUP, 2 * GROUP), 2 * GROUP)
-            mixed = mm(layer.mix[0, part], banks, (1, 0)) + mm(layer.mix[1, part], banks, (1, 0))
-            layer.kern_out[part, cols] = mixed.astype(BF16)
-
-        loop(0, 2, chunk)
+        mixed = mm(layer.mix[0, part], banks, (1, 0)) + mm(layer.mix[1, part], banks, (1, 0))
+        layer.kern_out[part, cols] = mixed.astype(BF16)
+
+    loop(0, 6, chunk)
+
+
+def send_kernels(layer, place):
+    mix_kernels(layer, place)
     send_rows(place, functools.partial(kern_copy, layer, place))
     own = rows_of(place.xy, ROWS)
     layer.kern_in[own, :] = layer.kern_out[own, :]
 
 
+class Samples:
+    def __init__(self, layer, place, scratch):
+        self.layer, self.place = layer, place
+        (
+            self.upstream, self.inputs, self.shifts, self.diff_out, self.diff_in,
+            self.up_ss, self.up_rs, self.in_ss, self.in_rs, self.diff_ss, self.diff_rs,
+        ) = scratch
+
+    def copy(self, source, target, send_sem, recv_sem, to):
+        return pltpu.make_async_remote_copy(
+            src_ref=source,
+            dst_ref=target,
+            send_sem=send_sem.at[0],
+            recv_sem=recv_sem.at[0],
+            device_id=self.place.at_xy(to),
+            device_id_type=MESH,
+        )
+
+    def up_copy(self, to):
+        return self.copy(self.layer.upstream, self.upstream.at[self.place.xy], self.up_ss, self.up_rs, to)
+
+    def in_copy(self, to):
+        rows, here = rows_of(to, ROWS), rows_of(self.place.xy, ROWS)
+        return self.copy(self.layer.flipped.at[rows], self.inputs.at[here], self.in_ss, self.in_rs, to)
+
+    def diff_copy(self, to):
+        rows, here = rows_of(to, ROWS), rows_of(self.place.xy, ROWS)
+        return self.copy(self.diff_out.at[rows], self.diff_in.at[here], self.diff_ss, self.diff_rs, to)
+
+    def all_copies(self):
+        to = (self.place.xy + 1) % N_XY
+        some, rows = pl.ds(0, N_XY - 1), pl.ds(0, (N_XY - 1) * ROWS)
+        return (
+            self.copy(self.upstream.at[some], self.upstream.at[some], self.up_ss, self.up_rs, to),
+            self.copy(self.layer.flipped.at[rows], self.inputs.at[rows], self.in_ss, self.in_rs, to),
+            self.copy(self.diff_out.at[rows], self.diff_in.at[rows], self.diff_ss, self.diff_rs, to),
+        )
+
+    def send(self):
+        place, own = self.place, rows_of(self.place.xy, ROWS)
+        load(self.layer, UPSTREAM).wait()
+        send_rows(place, self.up_copy)
+        flip_inputs(self.layer)
+        send_rows(place, self.in_copy)
+        self.upstream[place.xy] = self.layer.upstream[...]
+        self.inputs[own] = self.layer.flipped[own]
+
+    def work(self):
+        layer, place, side = self.layer, self.place, self.layer.side
+        pixels = side * side
+        for at in range(AT_ONCE):
+            clear_edges(self.shifts.at[at], side)
+        for copy in self.all_copies()[:2]:
+            copy.wait_recv()
+
+        def some(n):
+            for at in range(AT_ONCE):
+                for part in range(pixels // STEP):
+                    shift_rows(self.upstream.at[n * AT_ONCE + at], self.shifts.at[at], side, part)
+            for at in range(AT_ONCE):
+                rows = rows_of(n * AT_ONCE + at, ROWS)
+                inputs, diff = self.inputs[rows], None
+                for row_shift in range(3):
+                    cols = slice(row_shift * ROW3, (row_shift + 1) * ROW3)
+                    start = (2 - row_shift) * side
+                    shifted = self.shifts[at, start : start + pixels]
+                    grad = mm(inputs, shifted, (1, 0)) * (1.0 / side)
+                    layer.grad_in[rows, cols] = grad.astype(BF16)
+                    term = mm(layer.kern_out[rows, cols], shifted, (1, 1))
+                    diff = term if diff is None else diff + term
+                self.diff_out[rows] = diff.astype(BF16)
+
+        loop(0, N_XY // AT_ONCE, some)
+        send_rows(place, self.diff_copy)
+        own = rows_of(place.xy, ROWS)
+        self.diff_in[own] = self.diff_out[own]
+
+
 def send_parts(layer, place):
-    all_grads(layer, place).wait_recv()
-    for row_shift in range(3):
-        cols = slice(row_shift * ROW3, (row_shift + 1) * ROW3)
+    def some(n):
+        cols = rows_of(n, ROW3)
         grads = layer.grad_in[:, cols]
         total = mm(layer.back[0], grads, (1, 0)) + mm(layer.back[1], grads, (1, 0))
         total = total.reshape(N_Z, BLOCK, ROW3)
         layer.part[:, :, cols] = total
         layer.part_out[:, :, cols] = total.astype(BF16)
+
+    loop(0, 3, some)
     for kind in (0, 1, 2, 4):
         part_copy(layer, place, kind).start()
 
@@ -382,12 +496,18 @@
 
 
 def coef_sums(layer):
-    bank_rows = BANK_ROWS
-    cross = mm(layer.grad_in[...], layer.banks[...], (1, 1))
-    cross = jnp.where(diagonal(), cross, 0.0).reshape(N_XY, ROWS, bank_rows).sum(axis=1)
-    row = iota((bank_rows, GROUP), 0)
-    pick = ((row // OWN) % BANKS == iota((bank_rows, GROUP), 1)).astype(F32)
-    return mm(cross, pick, (1, 0), HIGH)
+    same = diagonal(STEP)
+
+    def some(n):
+        cross = mm(layer.grad_in[rows_of(n, STEP)], layer.banks[...], (1, 1))
+        cross = jnp.where(same, cross, 0.0).reshape(STEP // ROWS, ROWS, BANK_ROWS).sum(axis=1)
+        for sample in range(STEP // ROWS):
+            layer.cross[pl.ds(n * (STEP // ROWS) + sample, 1), :] = cross[sample : sample + 1]
+
+    loop(0, CHANNELS // STEP, some)
+    row = iota((BANK_ROWS, GROUP), 0)
+    pick = ((row // OWN) % BANKS == iota((BANK_ROWS, GROUP), 1)).astype(F32)
+    return mm(layer.cross[...], pick, (1, 0), HIGH)
 
 
 def diff_of(layer, place, chan):
@@ -401,26 +521,40 @@
     def _():
         many_kernels(layer, place, y, y * 4, 3).wait_recv()
 
-    part = pl.ds(pl.multiple_of(chan * GROUP, GROUP), GROUP)
-    diff = mm(window(layer, 0), layer.kern_in[part, 0:ROW3], (1, 1))
-    for row_shift in (1, 2):
-        cols = slice(row_shift * ROW3, (row_shift + 1) * ROW3)
-        diff = diff + mm(window(layer, row_shift), layer.kern_in[part, cols], (1, 1))
-    layer.diff[...] = diff
-
-
-def send_diffs(layer, place):
-    diff_of(layer, place, place.corner)
-    layer.diff_out[0] = layer.diff[...].astype(BF16)
-    diff_copy(layer, place, 0).start()
-    diff_of(layer, place, place.across)
-    diff_copy(layer, place, 0).wait_recv()
-    layer.diff_out[1] = (layer.diff[...] + layer.diff_in[0].astype(F32)).astype(BF16)
-    diff_copy(layer, place, 1).start()
-    diff_of(layer, place, place.sibling)
-    layer.diff_out[2] = layer.diff[...].astype(BF16)
-    diff_copy(layer, place, 2).start()
-    diff_of(layer, place, place.chan)
+    part, size = rows_of(chan, GROUP), 2 * STEP
+
+    def some(n):
+        diff = mm(window(layer, 0, n * size, size), layer.kern_in[part, 0:ROW3], (1, 1))
+        for row_shift in (1, 2):
+            cols = slice(row_shift * ROW3, (row_shift + 1) * ROW3)
+            diff = diff + mm(window(layer, row_shift, n * size, size), layer.kern_in[part, cols], (1, 1))
+        layer.diff[rows_of(n, size)] = diff
+
+    loop(0, layer.side * layer.side // size, some)
+
+
+def send_diffs(layer, place, diff_of):
+    def target(n):
+        base = (place.chan + 2 * (1 - n // 2)) % N_CHAN
+        diff_of(base + (1 - n % 2) * (1 - 2 * (place.chan % 2)))
+
+        @pl.when(n == 0)
+        def _():
+            layer.diff_out[0] = layer.diff[...].astype(BF16)
+            diff_copy(layer, place, 0).start()
+
+        @pl.when(n == 1)
+        def _():
+            diff_copy(layer, place, 0).wait_recv()
+            layer.diff_out[1] = (layer.diff[...] + layer.diff_in[0].astype(F32)).astype(BF16)
+            diff_copy(layer, place, 1).start()
+
+        @pl.when(n == 2)
+        def _():
+            layer.diff_out[2] = layer.diff[...].astype(BF16)
+            diff_copy(layer, place, 2).start()
+
+    loop(0, N_CHAN, target)
 
 
 def finish_update(layer, place):
@@ -437,7 +571,7 @@
     for kind in (2, 1):
         diff_copy(layer, place, kind).wait_recv()
         total = total + layer.diff_in[kind].astype(F32)
-    layer.delta[...] = total.astype(BF16)
+    layer.delta[...] = (total if layer.side == FINE_SIDE else total.T).astype(BF16)
 
 
 def finish_logit(layer, place, total):
@@ -450,9 +584,10 @@
     args, outs, scratch = refs[:8], refs[8:14], refs[14:]
     fine = Layer(FINE_SIDE, args[:4], *outs[:3], scratch[:N_LAYER_SCRATCH])
     coarse = Layer(COARSE_SIDE, args[4:], *outs[3:], scratch[N_LAYER_SCRATCH : 2 * N_LAYER_SCRATCH])
-    coef_out, coef_in, totals, coef_ss, coef_rs, total_ss, total_rs = scratch[2 * N_LAYER_SCRATCH :]
+    coef_out, coef_in, totals, coef_ss, coef_rs, total_ss, total_rs, *rest = scratch[2 * N_LAYER_SCRATCH :]
     layers = (fine, coarse)
     place = Place()
+    samples = Samples(coarse, place, rest)
 
     for which in (BANK, UPSTREAM, INPUTS, COEFS):
         for layer in layers:
@@ -474,41 +609,47 @@
     for layer in layers:
         for kind in (0, 1):
             bank_copy(layer, place, kind).start()
+    samples.send()
     send_grads(fine, place)
-    forward_bank(fine, place)
-    shift_upstream(coarse)
-    send_grads(coarse, place)
-    forward_bank(coarse, place)
+    for layer in layers:
+        forward_bank(layer, place)
     for layer in layers:
         spread_coefs(layer, place)
-    for layer in layers:
-        send_kernels(layer, place)
+    send_kernels(fine, place)
+    mix_kernels(coarse, place)
+    samples.work()
+    send_parts(coarse, place)
+    coarse_sums = coef_sums(coarse)
+    all_grads(fine, place).wait_recv()
     send_parts(fine, place)
+    relay_parts(coarse, place)
     fine_sums = coef_sums(fine)
-    send_parts(coarse, place)
-    relay_parts(fine, place)
-    coarse_sums = coef_sums(coarse)
     shape = (N_XY, 8, GROUP)
     wide_sums = [jnp.broadcast_to(sums[:, None, :], shape) for sums in (fine_sums, coarse_sums)]
     coef_out[...] = jnp.where(iota(shape, 1) == 0, *wide_sums)
     coef_refs = (coef_out, coef_in, coef_ss, coef_rs, place)
     loop(1, N_XY, lambda n: coef_copy(*coef_refs, (place.xy + n) % N_XY).start())
     coef_in[place.xy] = coef_out[place.xy]
-    relay_parts(coarse, place)
+    relay_parts(fine, place)
     all_coefs(*coef_refs).wait_recv()
     totals[place.chan] = coef_in[...].sum(axis=0)
     total_refs = (totals, total_ss, total_rs, place)
     loop(1, N_CHAN, lambda n: total_copy(*total_refs, (place.chan + n) % N_CHAN, place.chan).start())
-    send_diffs(fine, place)
-    for layer in layers:
-        finish_update(layer, place)
+    samples.all_copies()[2].wait_recv()
+
+    def coarse_diff(chan):
+        coarse.diff[...] = samples.diff_in[rows_of(chan, GROUP)].astype(F32)
+
+    send_diffs(coarse, place, coarse_diff)
+    finish_update(coarse, place)
     loop(1, N_CHAN, lambda n: total_copy(*total_refs, place.chan, (place.chan + n) % N_CHAN).wait_recv())
     total = totals[...].sum(axis=0)
     for index, layer in enumerate(layers):
         finish_logit(layer, place, total[index : index + 1, 0:BANKS])
-    send_diffs(coarse, place)
-    for layer in layers:
-        finish_delta(layer, place)
+    finish_update(fine, place)
+    finish_delta(coarse, place)
+    send_diffs(fine, place, functools.partial(diff_of, fine, place))
+    finish_delta(fine, place)
 
     for layer in layers:
         for kind in range(4):
@@ -517,8 +658,10 @@
             part_copy(layer, place, kind).wait_send()
         for kind in range(3):
             diff_copy(layer, place, kind).wait_send()
-        all_grads(layer, place).wait_send()
-        many_kernels(layer, place, 0, 0, N_XY - 1).wait_send()
+    all_grads(fine, place).wait_send()
+    many_kernels(fine, place, 0, 0, N_XY - 1).wait_send()
+    for copy in samples.all_copies():
+        copy.wait_send()
     all_coefs(*coef_refs).wait_send()
     loop(1, N_CHAN, lambda n: total_copy(*total_refs, (place.chan + n) % N_CHAN, place.chan).wait_send())
 
@@ -570,7 +713,13 @@
             pltpu.SemaphoreType.DMA((1,)),
             pltpu.SemaphoreType.DMA((N_CHAN,)),
             pltpu.SemaphoreType.DMA((N_CHAN,)),
-        ],
+            pltpu.VMEM((N_XY, COARSE_SIDE * COARSE_SIDE, GROUP), BF16),
+            pltpu.VMEM((CHANNELS, COARSE_SIDE * COARSE_SIDE), BF16),
+            pltpu.VMEM((AT_ONCE, COARSE_SIDE * COARSE_SIDE + 2 * COARSE_SIDE, ROW3), BF16),
+            pltpu.VMEM((CHANNELS, COARSE_SIDE * COARSE_SIDE), BF16),
+            pltpu.VMEM((CHANNELS, COARSE_SIDE * COARSE_SIDE), BF16),
+        ]
+        + [pltpu.SemaphoreType.DMA((1,))] * 6,
         compiler_params=pltpu.CompilerParams(
             collective_id=0, has_side_effects=True, vmem_limit_bytes=62 * MIB
         ),

time: 86 us -> 76 us (0.88)
  Pallas kernels: 85.2 us -> 75.2 us
    pallas_call x1, Pallas kernels: 83.2 us -> 73.3 us  [per_device(): pl.pallas_call(kernel, out_shape=out_shape, in_specs=[hbm] * 8, out_specs...]
where the time goes in v3:
time: 76 us; the launch traced here: 75.9 us
  Pallas kernels  75.2 us (99%)
    pallas_call x1, Pallas kernels, per_device(): pl.pallas_call(kernel, out_shape=out_shape, in_specs=[hbm] * 8, out_specs...  73.3 us
    pallas_call x1, Pallas kernels, per_device(): pl.pallas_call(store, out_shape=out_shape, in_specs=[hbm] * 6, out_specs=...  1.99 us

profile of v3, /device:TPU:1, one launch (start us, length us, event | category | flops | bytes accessed | tf_op | source)
XLA Modules:
  0.0 75.9 jit_solution(1201848884953879029)
XLA Ops:
  0.6 73.3 %shard_map.127 = (bf16[1024,128]{1,0:T(8,128)(2,1)}, f32[8,9,8,128]{3,2,1,0:T(8,128)}, f32[1,8]{1,0:T(1,128)}, bf16[256,128]{1,0:T(8,128)(2,1)}, f32[8,9,8,128]{3,2,1,0:T(8,128)}, /*index=5*/f32[1,8]{1,0:T(1,128)}) custom-call(bf16[1024,512]{1,0:T(8,128)(2,1)} %bitcast.8, bf16[1024,128]{1,0:T(8,128)(2,1)} %bitcast.9, bf16[8,9,8,128]{3,2,1,0:T(8,128)(2,1)} %refs_2_.1, ...), custom_call_target="tpu_custom_call" | custom-call | tf_op jit(solution)/shard_map/pallas_call | solution.py:701
  73.9 2.0 %shard_map.128 = (bf16[1024,128]{1,0:T(8,128)(2,1)}, f32[8,9,8,128]{3,2,1,0:T(8,128)}, f32[1,8]{1,0:T(1,128)}, bf16[256,128]{1,0:T(8,128)(2,1)}, f32[8,9,8,128]{3,2,1,0:T(8,128)}, /*index=5*/f32[1,8]{1,0:T(1,128)}) custom-call(bf16[1024,128]{1,0:T(8,128)(2,1)} %get-tuple-element.18.refs_0_, f32[8,9,8,128]{3,2,1,0:T(8,128)} %get-tuple-element.19.refs_1_, ...), custom_call_target="tpu_custom_call" | custom-call | tf_op jit(solution)/shard_map/pallas_call | solution.py:736

commit v4 on v3

--- a/solution.py
+++ b/solution.py
@@ -422,14 +422,14 @@
         rows, here = rows_of(to, ROWS), rows_of(self.place.xy, ROWS)
         return self.copy(self.diff_out.at[rows], self.diff_in.at[here], self.diff_ss, self.diff_rs, to)
 
-    def all_copies(self):
-        to = (self.place.xy + 1) % N_XY
+    def all_copies(self, which):
         some, rows = pl.ds(0, N_XY - 1), pl.ds(0, (N_XY - 1) * ROWS)
-        return (
-            self.copy(self.upstream.at[some], self.upstream.at[some], self.up_ss, self.up_rs, to),
-            self.copy(self.layer.flipped.at[rows], self.inputs.at[rows], self.in_ss, self.in_rs, to),
-            self.copy(self.diff_out.at[rows], self.diff_in.at[rows], self.diff_ss, self.diff_rs, to),
-        )
+        refs = (
+            (self.upstream.at[some], self.upstream.at[some], self.up_ss, self.up_rs),
+            (self.layer.flipped.at[rows], self.inputs.at[rows], self.in_ss, self.in_rs),
+            (self.diff_out.at[rows], self.diff_in.at[rows], self.diff_ss, self.diff_rs),
+        )[which]
+        return self.copy(*refs, (self.place.xy + 1) % N_XY)
 
     def send(self):
         place, own = self.place, rows_of(self.place.xy, ROWS)
@@ -440,34 +440,44 @@
         self.upstream[place.xy] = self.layer.upstream[...]
         self.inputs[own] = self.layer.flipped[own]
 
-    def work(self):
-        layer, place, side = self.layer, self.place, self.layer.side
-        pixels = side * side
-        for at in range(AT_ONCE):
-            clear_edges(self.shifts.at[at], side)
-        for copy in self.all_copies()[:2]:
-            copy.wait_recv()
-
+    def window(self, sample, row_shift):
+        side = self.layer.side
+        start = (2 - row_shift) * side
+        return self.shifts[sample, start : start + side * side]
+
+    def grads(self):
+        layer, side = self.layer, self.layer.side
+        self.all_copies(0).wait_recv()
+        self.all_copies(1).wait_recv()
+
+        def some(n):
+            picked = [n * AT_ONCE + at for at in range(AT_ONCE)]
+            for sample in picked:
+                clear_edges(self.shifts.at[sample], side)
+                for part in range(side * side // STEP):
+                    shift_rows(self.upstream.at[sample], self.shifts.at[sample], side, part)
+            for sample in picked:
+                rows = rows_of(sample, ROWS)
+                for row_shift in range(3):
+                    grad = mm(self.inputs[rows], self.window(sample, row_shift), (1, 0)) * (1.0 / side)
+                    layer.grad_in[rows, row_shift * ROW3 : (row_shift + 1) * ROW3] = grad.astype(BF16)
+
+        loop(0, N_XY // AT_ONCE, some)
+
+    def send_diffs(self):
         def some(n):
             for at in range(AT_ONCE):
-                for part in range(pixels // STEP):
-                    shift_rows(self.upstream.at[n * AT_ONCE + at], self.shifts.at[at], side, part)
-            for at in range(AT_ONCE):
-                rows = rows_of(n * AT_ONCE + at, ROWS)
-                inputs, diff = self.inputs[rows], None
+                sample = n * AT_ONCE + at
+                rows, diff = rows_of(sample, ROWS), None
                 for row_shift in range(3):
                     cols = slice(row_shift * ROW3, (row_shift + 1) * ROW3)
-                    start = (2 - row_shift) * side
-                    shifted = self.shifts[at, start : start + pixels]
-                    grad = mm(inputs, shifted, (1, 0)) * (1.0 / side)
-                    layer.grad_in[rows, cols] = grad.astype(BF16)
-                    term = mm(layer.kern_out[rows, cols], shifted, (1, 1))
+                    term = mm(self.layer.kern_out[rows, cols], self.window(sample, row_shift), (1, 1))
                     diff = term if diff is None else diff + term
                 self.diff_out[rows] = diff.astype(BF16)
 
         loop(0, N_XY // AT_ONCE, some)
-        send_rows(place, self.diff_copy)
-        own = rows_of(place.xy, ROWS)
+        send_rows(self.place, self.diff_copy)
+        own = rows_of(self.place.xy, ROWS)
         self.diff_in[own] = self.diff_out[own]
 
 
@@ -611,18 +621,19 @@
             bank_copy(layer, place, kind).start()
     samples.send()
     send_grads(fine, place)
-    for layer in layers:
-        forward_bank(layer, place)
+    forward_bank(fine, place)
     for layer in layers:
         spread_coefs(layer, place)
+    forward_bank(coarse, place)
     send_kernels(fine, place)
+    samples.grads()
+    send_parts(coarse, place)
     mix_kernels(coarse, place)
-    samples.work()
-    send_parts(coarse, place)
+    samples.send_diffs()
+    relay_parts(coarse, place)
     coarse_sums = coef_sums(coarse)
     all_grads(fine, place).wait_recv()
     send_parts(fine, place)
-    relay_parts(coarse, place)
     fine_sums = coef_sums(fine)
     shape = (N_XY, 8, GROUP)
     wide_sums = [jnp.broadcast_to(sums[:, None, :], shape) for sums in (fine_sums, coarse_sums)]
@@ -630,25 +641,25 @@
     coef_refs = (coef_out, coef_in, coef_ss, coef_rs, place)
     loop(1, N_XY, lambda n: coef_copy(*coef_refs, (place.xy + n) % N_XY).start())
     coef_in[place.xy] = coef_out[place.xy]
+    samples.all_copies(2).wait_recv()
+
+    def coarse_diff(chan):
+        coarse.diff[...] = samples.diff_in[rows_of(chan, GROUP)].astype(F32)
+
+    send_diffs(coarse, place, coarse_diff)
     relay_parts(fine, place)
     all_coefs(*coef_refs).wait_recv()
     totals[place.chan] = coef_in[...].sum(axis=0)
     total_refs = (totals, total_ss, total_rs, place)
     loop(1, N_CHAN, lambda n: total_copy(*total_refs, (place.chan + n) % N_CHAN, place.chan).start())
-    samples.all_copies()[2].wait_recv()
-
-    def coarse_diff(chan):
-        coarse.diff[...] = samples.diff_in[rows_of(chan, GROUP)].astype(F32)
-
-    send_diffs(coarse, place, coarse_diff)
+    send_diffs(fine, place, functools.partial(diff_of, fine, place))
     finish_update(coarse, place)
+    finish_delta(coarse, place)
     loop(1, N_CHAN, lambda n: total_copy(*total_refs, place.chan, (place.chan + n) % N_CHAN).wait_recv())
     total = totals[...].sum(axis=0)
     for index, layer in enumerate(layers):
         finish_logit(layer, place, total[index : index + 1, 0:BANKS])
     finish_update(fine, place)
-    finish_delta(coarse, place)
-    send_diffs(fine, place, functools.partial(diff_of, fine, place))
     finish_delta(fine, place)
 
     for layer in layers:
@@ -660,8 +671,8 @@
             diff_copy(layer, place, kind).wait_send()
     all_grads(fine, place).wait_send()
     many_kernels(fine, place, 0, 0, N_XY - 1).wait_send()
-    for copy in samples.all_copies():
-        copy.wait_send()
+    for which in range(3):
+        samples.all_copies(which).wait_send()
     all_coefs(*coef_refs).wait_send()
     loop(1, N_CHAN, lambda n: total_copy(*total_refs, (place.chan + n) % N_CHAN, place.chan).wait_send())
 
@@ -715,7 +726,7 @@
             pltpu.SemaphoreType.DMA((N_CHAN,)),
             pltpu.VMEM((N_XY, COARSE_SIDE * COARSE_SIDE, GROUP), BF16),
             pltpu.VMEM((CHANNELS, COARSE_SIDE * COARSE_SIDE), BF16),
-            pltpu.VMEM((AT_ONCE, COARSE_SIDE * COARSE_SIDE + 2 * COARSE_SIDE, ROW3), BF16),
+            pltpu.VMEM((N_XY, COARSE_SIDE * COARSE_SIDE + 2 * COARSE_SIDE, ROW3), BF16),
             pltpu.VMEM((CHANNELS, COARSE_SIDE * COARSE_SIDE), BF16),
             pltpu.VMEM((CHANNELS, COARSE_SIDE * COARSE_SIDE), BF16),
         ]

time: 76 us -> 73.8 us (0.971)
  Pallas kernels: 75.2 us -> 73 us
    pallas_call x1, Pallas kernels: 73.3 us -> 71 us  [per_device(): pl.pallas_call(kernel, out_shape=out_shape, in_specs=[hbm] * 8, out_specs...]
where the time goes in v4:
time: 73.8 us; the launch traced here: 73.6 us
  Pallas kernels  73 us (99%)
    pallas_call x1, Pallas kernels, per_device(): pl.pallas_call(kernel, out_shape=out_shape, in_specs=[hbm] * 8, out_specs...  71 us
    pallas_call x1, Pallas kernels, per_device(): pl.pallas_call(store, out_shape=out_shape, in_specs=[hbm] * 6, out_specs=...  1.99 us

profile of v4, /device:TPU:1, one launch (start us, length us, event | category | flops | bytes accessed | tf_op | source)
XLA Modules:
  0.0 73.6 jit_solution(1393859258156505139)
XLA Ops:
  0.6 71.0 %shard_map.127 = (bf16[1024,128]{1,0:T(8,128)(2,1)}, f32[8,9,8,128]{3,2,1,0:T(8,128)}, f32[1,8]{1,0:T(1,128)}, bf16[256,128]{1,0:T(8,128)(2,1)}, f32[8,9,8,128]{3,2,1,0:T(8,128)}, /*index=5*/f32[1,8]{1,0:T(1,128)}) custom-call(bf16[1024,512]{1,0:T(8,128)(2,1)} %bitcast.8, bf16[1024,128]{1,0:T(8,128)(2,1)} %bitcast.9, bf16[8,9,8,128]{3,2,1,0:T(8,128)(2,1)} %refs_2_.1, ...), custom_call_target="tpu_custom_call" | custom-call | tf_op jit(solution)/shard_map/pallas_call | solution.py:712
  71.7 2.0 %shard_map.128 = (bf16[1024,128]{1,0:T(8,128)(2,1)}, f32[8,9,8,128]{3,2,1,0:T(8,128)}, f32[1,8]{1,0:T(1,128)}, bf16[256,128]{1,0:T(8,128)(2,1)}, f32[8,9,8,128]{3,2,1,0:T(8,128)}, /*index=5*/f32[1,8]{1,0:T(1,128)}) custom-call(bf16[1024,128]{1,0:T(8,128)(2,1)} %get-tuple-element.18.refs_0_, f32[8,9,8,128]{3,2,1,0:T(8,128)} %get-tuple-element.19.refs_1_, ...), custom_call_target="tpu_custom_call" | custom-call | tf_op jit(solution)/shard_map/pallas_call | solution.py:747

commit v5 on v4

--- a/solution.py
+++ b/solution.py
@@ -646,8 +646,8 @@
     def coarse_diff(chan):
         coarse.diff[...] = samples.diff_in[rows_of(chan, GROUP)].astype(F32)
 
+    relay_parts(fine, place)
     send_diffs(coarse, place, coarse_diff)
-    relay_parts(fine, place)
     all_coefs(*coef_refs).wait_recv()
     totals[place.chan] = coef_in[...].sum(axis=0)
     total_refs = (totals, total_ss, total_rs, place)

time: 73.8 us -> 72.6 us (0.984)
  Pallas kernels: 73 us -> 71.8 us
    pallas_call x1, Pallas kernels: 71 us -> 69.8 us  [per_device(): pl.pallas_call(kernel, out_shape=out_shape, in_specs=[hbm] * 8, out_specs...]
where the time goes in v5:
time: 72.6 us; the launch traced here: 72.4 us
  Pallas kernels  71.8 us (99%)
    pallas_call x1, Pallas kernels, per_device(): pl.pallas_call(kernel, out_shape=out_shape, in_specs=[hbm] * 8, out_specs...  69.8 us
    pallas_call x1, Pallas kernels, per_device(): pl.pallas_call(store, out_shape=out_shape, in_specs=[hbm] * 6, out_specs=...  1.99 us

profile of v5, /device:TPU:1, one launch (start us, length us, event | category | flops | bytes accessed | tf_op | source)
XLA Modules:
  0.0 72.4 jit_solution(13169343855779690399)
XLA Ops:
  0.6 69.8 %shard_map.127 = (bf16[1024,128]{1,0:T(8,128)(2,1)}, f32[8,9,8,128]{3,2,1,0:T(8,128)}, f32[1,8]{1,0:T(1,128)}, bf16[256,128]{1,0:T(8,128)(2,1)}, f32[8,9,8,128]{3,2,1,0:T(8,128)}, /*index=5*/f32[1,8]{1,0:T(1,128)}) custom-call(bf16[1024,512]{1,0:T(8,128)(2,1)} %bitcast.8, bf16[1024,128]{1,0:T(8,128)(2,1)} %bitcast.9, bf16[8,9,8,128]{3,2,1,0:T(8,128)(2,1)} %refs_2_.1, ...), custom_call_target="tpu_custom_call" | custom-call | tf_op jit(solution)/shard_map/pallas_call | solution.py:712
  70.4 2.0 %shard_map.128 = (bf16[1024,128]{1,0:T(8,128)(2,1)}, f32[8,9,8,128]{3,2,1,0:T(8,128)}, f32[1,8]{1,0:T(1,128)}, bf16[256,128]{1,0:T(8,128)(2,1)}, f32[8,9,8,128]{3,2,1,0:T(8,128)}, /*index=5*/f32[1,8]{1,0:T(1,128)}) custom-call(bf16[1024,128]{1,0:T(8,128)(2,1)} %get-tuple-element.18.refs_0_, f32[8,9,8,128]{3,2,1,0:T(8,128)} %get-tuple-element.19.refs_1_, ...), custom_call_target="tpu_custom_call" | custom-call | tf_op jit(solution)/shard_map/pallas_call | solution.py:747

commit v6 on v5

--- a/solution.py
+++ b/solution.py
@@ -635,6 +635,7 @@
     all_grads(fine, place).wait_recv()
     send_parts(fine, place)
     fine_sums = coef_sums(fine)
+    relay_parts(fine, place)
     shape = (N_XY, 8, GROUP)
     wide_sums = [jnp.broadcast_to(sums[:, None, :], shape) for sums in (fine_sums, coarse_sums)]
     coef_out[...] = jnp.where(iota(shape, 1) == 0, *wide_sums)
@@ -646,7 +647,6 @@
     def coarse_diff(chan):
         coarse.diff[...] = samples.diff_in[rows_of(chan, GROUP)].astype(F32)
 
-    relay_parts(fine, place)
     send_diffs(coarse, place, coarse_diff)
     all_coefs(*coef_refs).wait_recv()
     totals[place.chan] = coef_in[...].sum(axis=0)

time: 72.6 us -> 72.5 us (level)
  no operation moved by 1% of the time
where the time goes in v6:
time: 72.5 us; the launch traced here: 72.4 us
  Pallas kernels  71.8 us (99%)
    pallas_call x1, Pallas kernels, per_device(): pl.pallas_call(kernel, out_shape=out_shape, in_specs=[hbm] * 8, out_specs...  69.8 us
    pallas_call x1, Pallas kernels, per_device(): pl.pallas_call(store, out_shape=out_shape, in_specs=[hbm] * 6, out_specs=...  1.99 us

profile of v6, /device:TPU:1, one launch (start us, length us, event | category | flops | bytes accessed | tf_op | source)
XLA Modules:
  0.0 72.4 jit_solution(12793929461721422342)
XLA Ops:
  0.6 69.8 %shard_map.127 = (bf16[1024,128]{1,0:T(8,128)(2,1)}, f32[8,9,8,128]{3,2,1,0:T(8,128)}, f32[1,8]{1,0:T(1,128)}, bf16[256,128]{1,0:T(8,128)(2,1)}, f32[8,9,8,128]{3,2,1,0:T(8,128)}, /*index=5*/f32[1,8]{1,0:T(1,128)}) custom-call(bf16[1024,512]{1,0:T(8,128)(2,1)} %bitcast.8, bf16[1024,128]{1,0:T(8,128)(2,1)} %bitcast.9, bf16[8,9,8,128]{3,2,1,0:T(8,128)(2,1)} %refs_2_.1, ...), custom_call_target="tpu_custom_call" | custom-call | tf_op jit(solution)/shard_map/pallas_call | solution.py:712
  70.4 2.0 %shard_map.128 = (bf16[1024,128]{1,0:T(8,128)(2,1)}, f32[8,9,8,128]{3,2,1,0:T(8,128)}, f32[1,8]{1,0:T(1,128)}, bf16[256,128]{1,0:T(8,128)(2,1)}, f32[8,9,8,128]{3,2,1,0:T(8,128)}, /*index=5*/f32[1,8]{1,0:T(1,128)}) custom-call(bf16[1024,128]{1,0:T(8,128)(2,1)} %get-tuple-element.18.refs_0_, f32[8,9,8,128]{3,2,1,0:T(8,128)} %get-tuple-element.19.refs_1_, ...), custom_call_target="tpu_custom_call" | custom-call | tf_op jit(solution)/shard_map/pallas_call | solution.py:747
